TPU v7x, 32 devices: a whole 2x2x4 slice. The times are simulated.
32 devices in a mesh: gx: 4 (over y, core), gy: 8 (over z, x).
Axes of the slice: x: 2, y: 2, z: 4, core: 2. Of those that a mesh axis runs over, the one named last changes fastest.
Arguments:
- right_side: float32 [128, 256, 256], P('gx', 'gy'), may hold values from -32 to 32
- phase: int32 [128, 256, 256], P('gx', 'gy'), may hold values from 1 to 3
- table: float32 [4], replicated, may hold values from 0.3 to 3
Outputs:
- solution_field: float32 [128, 256, 256], P('gx', 'gy')
- residual: float32 [128, 256, 256], P('gx', 'gy')
- pre_residual: float32 [128, 256, 256], P('gx', 'gy')
- residual_image: float32 [128, 256, 256], P('gx', 'gy')
Inputs may be any that keep to these rules, and one draw needn't show every extreme that they name: `phase`: labels 1 slag, 2 steel, 3 argon plume; label 0 stands for the lining outside the grid.
All inputs are finite; a program needn't handle non-finite values.
Results may differ from a plain program's by a relative error of at most 0.0003.
Values sent between devices are 32-bit elements; how exact they have to be, the bound alone decides.
A program may use at most 64 MiB of HBM per device.

v0:
```python
import jax
import jax.numpy as jnp
from jax import lax
from jax.sharding import PartitionSpec as P

ITERS = 2


centre_value = 1.1
half_width = 0.9
ratio_sigma = centre_value / half_width
rho_first = 1.0 / ratio_sigma
rho_second = 1.0 / (2.0 * ratio_sigma - rho_first)
rho_third = 1.0 / (2.0 * ratio_sigma - rho_second)
start_scale = 1.0 / centre_value
keep_first = rho_second * rho_first
push_first = 2.0 * rho_second / half_width
keep_second = rho_third * rho_second
push_second = 2.0 * rho_third / half_width


def extended_2(block, sides, width):
    for axis, dim in sides:
        count = lax.axis_size(axis)
        forward = [(i, i + 1) for i in range(count - 1)]
        backward = [(target, source) for source, target in forward]
        low = lax.ppermute(
            lax.slice_in_dim(block, block.shape[dim] - width, None, axis=dim), axis, forward
        )
        high = lax.ppermute(lax.slice_in_dim(block, 0, width, axis=dim), axis, backward)
        block = jnp.concatenate([low, block, high], axis=dim)
    return block


def harmonic(left, right):
    return 2.0 * left * right / (left + right)


def coupling_set(sigma_padded):
    centre = sigma_padded[1:-1, 1:-1, 1:-1]
    to_west = harmonic(centre, sigma_padded[:-2, 1:-1, 1:-1])
    to_east = harmonic(centre, sigma_padded[2:, 1:-1, 1:-1])
    to_south = harmonic(centre, sigma_padded[1:-1, :-2, 1:-1])
    to_north = harmonic(centre, sigma_padded[1:-1, 2:, 1:-1])
    to_down = harmonic(centre, sigma_padded[1:-1, 1:-1, :-2])
    to_up = harmonic(centre, sigma_padded[1:-1, 1:-1, 2:])
    diagonal = to_west + to_east + to_south + to_north + to_down + to_up
    return (to_west, to_east, to_south, to_north, to_down, to_up, diagonal)


def shrink(field, amount):
    if amount == 0:
        return field
    return field[amount:-amount, amount:-amount]


def lookup(labels, table):
    return jnp.where(
        labels == 1,
        table[1],
        jnp.where(labels == 2, table[2], jnp.where(labels == 3, table[3], table[0])),
    )


def operate_ext(padded_xy, couplings):
    to_west, to_east, to_south, to_north, to_down, to_up, diagonal = couplings
    padded_z = jnp.pad(padded_xy, ((0, 0), (0, 0), (1, 1)))
    centre = padded_xy[1:-1, 1:-1]
    beside = (
        to_west * padded_xy[:-2, 1:-1]
        + to_east * padded_xy[2:, 1:-1]
        + to_south * padded_xy[1:-1, :-2]
        + to_north * padded_xy[1:-1, 2:]
        + to_down * padded_z[1:-1, 1:-1, :-2]
        + to_up * padded_z[1:-1, 1:-1, 2:]
    )
    return diagonal * centre - beside


def local(right_side, phase, table):
    cells_x, cells_y, cells_z = right_side.shape
    depth = 3
    labels_ext = extended_2(phase, (("gx", 0), ("gy", 1)), 4)
    sigma_ext = lookup(jnp.pad(labels_ext, ((0, 0), (0, 0), (1, 1))), table)
    stored_set = coupling_set(sigma_ext)

    def couplings_at(cycle):
        return tuple((shrink(member, depth - cycle) for member in stored_set))

    def mask_at(cycle):
        row_index = (
            lax.axis_index("gx") * cells_x
            + jnp.arange(cells_x + 2 * cycle, dtype=jnp.int32)
            - cycle
        )
        col_index = (
            lax.axis_index("gy") * cells_y
            + jnp.arange(cells_y + 2 * cycle, dtype=jnp.int32)
            - cycle
        )
        rows_in = ((row_index >= 0) & (row_index < cells_x * lax.axis_size("gx"))).astype(
            jnp.float32
        )
        cols_in = ((col_index >= 0) & (col_index < cells_y * lax.axis_size("gy"))).astype(
            jnp.float32
        )
        return rows_in[:, None, None] * cols_in[None, :, None]

    def composite(vector):
        extended = extended_2(vector, (("gx", 0), ("gy", 1)), 3)
        set_three = couplings_at(3)
        first = start_scale * (extended / set_three[6])
        set_two = couplings_at(2)
        remain = shrink(extended, 1) - operate_ext(first, set_two)
        change = (keep_first * shrink(first, 1) + push_first * (remain / set_two[6])) * mask_at(2)
        second = shrink(first, 1) + change
        set_one = couplings_at(1)
        remain = shrink(extended, 2) - operate_ext(second, set_one)
        change = (keep_second * shrink(change, 1) + push_second * (remain / set_one[6])) * mask_at(
            1
        )
        third = shrink(second, 1) + change
        return (shrink(third, 1), operate_ext(third, couplings_at(0)))

    solution_field = jnp.zeros_like(right_side)
    residual = right_side
    pre_residual, residual_image = composite(residual)
    image_dir = jnp.zeros_like(right_side)
    pre_dir = jnp.zeros_like(right_side)
    resid_dir = jnp.zeros_like(right_side)
    direction = jnp.zeros_like(right_side)
    energy_prev = jnp.float32(1.0)
    step_prev = jnp.float32(1.0)
    for iteration in range(ITERS):
        energy_now, curvature = lax.psum(
            (jnp.sum(residual * pre_residual), jnp.sum(residual_image * pre_residual)), ("gx", "gy")
        )
        pre_image, double_image = composite(residual_image)
        if iteration == 0:
            step_size = energy_now / curvature
            image_dir = double_image
            pre_dir = pre_image
            resid_dir = residual_image
            direction = pre_residual
        else:
            momentum = energy_now / energy_prev
            step_size = energy_now / (curvature - momentum * energy_now / step_prev)
            image_dir = double_image + momentum * image_dir
            pre_dir = pre_image + momentum * pre_dir
            resid_dir = residual_image + momentum * resid_dir
            direction = pre_residual + momentum * direction
        solution_field = solution_field + step_size * direction
        residual = residual - step_size * resid_dir
        pre_residual = pre_residual - step_size * pre_dir
        residual_image = residual_image - step_size * image_dir
        energy_prev = energy_now
        step_prev = step_size
    return (solution_field, residual, pre_residual, residual_image)


def solution(mesh):
    placed = (P("gx", "gy", None), P("gx", "gy", None), P())
    return jax.shard_map(
        local,
        mesh=mesh,
        in_specs=placed,
        out_specs=(
            P("gx", "gy", None),
            P("gx", "gy", None),
            P("gx", "gy", None),
            P("gx", "gy", None),
        ),
        check_vma=False,
    )
```

profile of v0, /device:TPU:0, one launch (start us, length us, event | category | flops | bytes accessed | tf_op | source)
XLA Modules:
  0.0 213.4 jit_solution(10288331728430111048)
XLA Ops:
  3.0 3.0 %collective-permute-start = (f32[3,32,256]{2,1,0:T(8,128)S(1)}, f32[3,32,256]{2,1,0:T(8,128)S(1)}, u32[]{:S(2)}, u32[]{:S(2)}) collective-permute-start(f32[3,32,256]{2,1,0:T(8,128)S(1)} %get-tuple-element.52), channel_id=1, source_target_pairs={{0,8},{8,16},{16,24},{1,9},{9,17},{17,25},{2,10},{10,18},{18,26},{... | collective-permute-start | bytes 294920 | tf_op jit(solution)/shard_map/ppermute | solution.py:27
  8.5 5.1 %collective-permute-start.4 = (s32[4,32,256]{2,1,0:T(8,128)S(1)}, s32[4,32,256]{2,1,0:T(8,128)S(1)}, u32[]{:S(2)}, u32[]{:S(2)}) collective-permute-start(s32[4,32,256]{2,1,0:T(8,128)S(1)} %get-tuple-element.50), channel_id=1, source_target_pairs={{0,8},{8,16},{16,24},{1,9},{9,17},{17,25},{2,10},{10,18},{18,26},{... | collective-permute-start | bytes 393224 | tf_op jit(solution)/shard_map/ppermute | solution.py:27
  15.5 3.4 %collective-permute-start.6 = (s32[40,4,256]{2,1,0:T(4,128)S(1)}, s32[40,4,256]{2,1,0:T(4,128)S(1)}, u32[]{:S(2)}, u32[]{:S(2)}) collective-permute-start(s32[40,4,256]{2,1,0:T(4,128)S(1)} %get-tuple-element.35), channel_id=1, source_target_pairs={{0,1},{1,2},{2,3},{3,4},{4,5},{5,6},{6,7},{8,9},{9,10},{10,11},{11... | collective-permute-start | bytes 491528 | tf_op jit(solution)/shard_map/ppermute | solution.py:27
  20.3 4.6 %collective-permute-start.2 = (f32[38,3,256]{2,1,0:T(4,128)S(1)}, f32[38,3,256]{2,1,0:T(4,128)S(1)}, u32[]{:S(2)}, u32[]{:S(2)}) collective-permute-start(f32[38,3,256]{2,1,0:T(4,128)S(1)} %get-tuple-element.41), channel_id=1, source_target_pairs={{0,1},{1,2},{2,3},{3,4},{4,5},{5,6},{6,7},{8,9},{9,10},{10,11},{11... | collective-permute-start | bytes 350216 | tf_op jit(solution)/shard_map/ppermute | solution.py:27
  27.5 3.3 %select_select_fusion = f32[40,40,258]{2,1,0:T(8,128)S(1)} fusion(s32[40,40,256]{2,1,0:T(8,128)S(1)} %pad_add_fusion, f32[]{:T(128)} %bitcast.3, f32[]{:T(128)} %bitcast.2, f32[]{:T(128)} %bitcast.1, f32[]{:T(128)} %bitcast), kind=kLoop, calls=%fused_computation.9 | loop fusion | flops 2476800 | bytes 3289616 | tf_op jit(solution)/shard_map/jit(_where)/select_n | solution.py:58
  31.2 2.6 %collective-permute-done.3 = f32[38,3,256]{2,1,0:T(4,128)S(1)} collective-permute-done((f32[38,3,256]{2,1,0:T(4,128)S(1)}, f32[38,3,256]{2,1,0:T(4,128)S(1)}, u32[]{:S(2)}, u32[]{:S(2)}) %collective-permute-start.3) | collective-permute-done | bytes 116768 | tf_op jit(solution)/shard_map/ppermute | solution.py:30
  33.8 3.4 %divide_multiply_fusion.2 = (f32[38,38,256]{2,1,0:T(8,128)S(1)}, f32[38,38,256]{2,1,0:T(8,128)S(1)}, f32[38,38,256]{2,1,0:T(8,128)S(1)}, f32[38,38,256]{2,1,0:T(...) fusion(f32[38,3,256]{2,1,0:T(4,128)S(1)} %collective-permute-do, ...), kind=kLoop, calls=%fused_computation.28 | loop fusion | flops 10350592 | bytes 25137152 | tf_op jit(solution)/shard_map/mul | solution.py:112
  37.3 3.6 %slice_add_fusion.2 = (f32[36,36,256]{2,1,0:T(8,128)S(1)}, f32[36,36,256]{2,1,0:T(8,128)S(1)}) fusion(f32[38,38,256]{2,1,0:T(8,128)S(1)} %get-tuple-element.22, f32[36,36]{1,0:T(8,128)S(1)} %broadcast_multiply_fusion.1, f32[38,38,256]{2,1,0:T(8,128)S(1)} %get-tuple-element.29, f32[38,38,256]{2,1,0:T(8,128)S(1)} %get-tuple-element.28, ...), kind=kLoop, calls=%fused_computation.137 | loop fusion | flops 6635520 | bytes 23400448 | tf_op jit(solution)/shard_map/add | solution.py:116
  40.9 3.4 %fusion.68 = f32[34,34,256]{2,1,0:T(8,128)S(1)} fusion(f32[36,36,256]{2,1,0:T(8,128)S(1)} %get-tuple-element.21, f32[36,36,256]{2,1,0:T(8,128)S(1)} %get-tuple-element.20, f32[38,38,256]{2,1,0:T(8,128)S(1)} %get-tuple-element.34, f32[38,38,256]{2,1,0:T(8,128)S(1)} %get-tuple-element.29, f32[38,38,256]{2,1,0:T(8,128)S(1)} %get-tuple-element.28, ...), kind=kLoop, calls=%fused_computation.134 | loop fusion | flops 5918720 | bytes 22175744 | tf_op jit(solution)/shard_map/add | solution.py:122
  44.4 4.8 %multiply_reduce_fusion.2 = (f32[]{:T(128)}, f32[]{:T(128)}, f32[32,32,256]{2,1,0:T(8,128)}) fusion(f32[34,34,256]{2,1,0:T(8,128)S(1)} %fusion.68, f32[32,32,256]{2,1,0:T(8,128)} %param.3, f32[38,38,256]{2,1,0:T(8,128)S(1)} %get-tuple-element.29, f32[38,38,256]{2,1,0:T(8,128)S(1)} %get-tuple-element.28, f32[38,38,256]{2,1,0:T(8,128)S(1)} %get-tuple-element.27, ...), kind=kLoop, calls=%fused_computation.185 | loop fusion | flops 4456446 | bytes 16072712 | tf_op jit(solution)/shard_map/reduce_sum | solution.py:136
  50.2 2.0 collective-permute-start.8
  53.5 4.3 %collective-permute-done.9 = f32[3,32,256]{2,1,0:T(8,128)S(1)} collective-permute-done((f32[3,32,256]{2,1,0:T(8,128)S(1)}, f32[3,32,256]{2,1,0:T(8,128)S(1)}, u32[]{:S(2)}, u32[]{:S(2)}) %collective-permute-start.9) | collective-permute-done | bytes 98336 | tf_op jit(solution)/shard_map/ppermute | solution.py:30
  59.6 4.8 %collective-permute-start.10 = (f32[38,3,256]{2,1,0:T(4,128)}, f32[38,3,256]{2,1,0:T(4,128)S(1)}, u32[]{:S(2)}, u32[]{:S(2)}) collective-permute-start(f32[38,3,256]{2,1,0:T(4,128)} %get-tuple-element.39), channel_id=1, source_target_pairs={{0,1},{1,2},{2,3},{3,4},{4,5},{5,6},{6,7},{8,9},{9,10},{10,11},{11... | collective-permute-start | bytes 350216 | tf_op jit(solution)/shard_map/ppermute | solution.py:27
  65.7 43.8 %all-reduce.11 = (f32[]{:T(128)}, f32[]{:T(128)}) all-reduce(f32[]{:T(128)} %get-tuple-element.5, f32[]{:T(128)} %get-tuple-element.4), channel_id=1, replica_groups=mesh['gx'=4,'gy'=8] {'gx','gy'}, use_global_device_ids=true, to_apply=%region_1.2 | all-reduce | flops 2 | bytes 16 | tf_op jit(solution)/shard_map/psum | solution.py:135
  114.0 4.8 %slice_add_fusion.1 = (f32[36,36,256]{2,1,0:T(8,128)S(1)}, f32[36,36,256]{2,1,0:T(8,128)S(1)}) fusion(f32[38,38,256]{2,1,0:T(8,128)S(1)} %get-tuple-element.33, f32[36,36]{1,0:T(8,128)S(1)} %broadcast_multiply_fusion.1, f32[38,38,256]{2,1,0:T(8,128)} %copy-done.12, f32[38,38,256]{2,1,0:T(8,128)S(1)} %copy-done.10, f32[38,38,256]{2,1,0:T(8,128)S(1)} %copy-done.7, ...), kind=kLoop, calls=%fused_computation.136 | loop fusion | flops 6635520 | bytes 23252992 | tf_op jit(solution)/shard_map/add | solution.py:116
  118.8 3.5 %fusion.62 = f32[34,34,256]{2,1,0:T(8,128)S(1)} fusion(f32[36,36,256]{2,1,0:T(8,128)S(1)} %get-tuple-element.19, f32[36,36,256]{2,1,0:T(8,128)S(1)} %get-tuple-element.18, f32[38,38,256]{2,1,0:T(8,128)S(1)} %get-tuple-element.32, f32[38,38,256]{2,1,0:T(8,128)S(1)} %copy-done.13, f32[38,38,256]{2,1,0:T(8,128)S(1)} %copy-done.10, ...), kind=kLoop, calls=%fused_computation.123 | loop fusion | flops 5918720 | bytes 22175744 | tf_op jit(solution)/shard_map/add | solution.py:122
  122.4 4.2 %multiply_reduce_fusion = (f32[]{:T(128)}, f32[]{:T(128)}, f32[32,32,256]{2,1,0:T(8,128)S(1)}, f32[32,32,256]{2,1,0:T(8,128)}, f32[32,32,256]{2,1,0:T(8,128)}) fusion(f32[32,32,256]{2,1,0:T(8,128)S(1)} %copy-done.23, f32[32,32,256]{2,1,0:T(8,128)S(1)} %copy-done.18, f32[]{:T(128)S(6)} %div.66, f32[38,38,256]{2,1,0:T(8,128)S(1)} %copy-done.13, ...), kind=kLoop, calls=%fused_computation.180 | loop fusion | flops 6029310 | bytes 20267020 | tf_op jit(solution)/shard_map/reduce_sum | solution.py:136
  130.2 45.0 %all-reduce.10 = (f32[]{:T(128)}, f32[]{:T(128)}) all-reduce(f32[]{:T(128)} %get-tuple-element.7, f32[]{:T(128)} %get-tuple-element.6), channel_id=1, replica_groups=mesh['gx'=4,'gy'=8] {'gx','gy'}, use_global_device_ids=true, to_apply=%region_5.6 | all-reduce | flops 2 | bytes 16 | tf_op jit(solution)/shard_map/psum | solution.py:135
  180.7 4.2 %collective-permute-start.14 = (f32[38,3,256]{2,1,0:T(4,128)S(1)}, f32[38,3,256]{2,1,0:T(4,128)S(1)}, u32[]{:S(2)}, u32[]{:S(2)}) collective-permute-start(f32[38,3,256]{2,1,0:T(4,128)S(1)} %get-tuple-element.37), channel_id=1, source_target_pairs={{0,1},{1,2},{2,3},{3,4},{4,5},{5,6},{6,7},{8,9},{9,10},{10,11},{11... | collective-permute-start | bytes 350216 | tf_op jit(solution)/shard_map/ppermute | solution.py:27
  186.5 3.0 %multiply_subtract_fusion.1 = f32[32,32,256]{2,1,0:T(8,128)} fusion(f32[32,32,256]{2,1,0:T(8,128)} %copy-done.20, f32[32,32,256]{2,1,0:T(8,128)S(1)} %copy-done.19, f32[32,32,256]{2,1,0:T(8,128)} %param.3, f32[]{:T(128)S(6)} %div.70, f32[]{:T(128)S(6)} %div.72, f32[]{:T(128)S(6)} %div.66), kind=kLoop, calls=%fused_computation.178 | loop fusion | flops 1572864 | bytes 4194316 | tf_op jit(solution)/shard_map/sub | solution.py:153
  192.5 3.6 %slice_add_fusion = (f32[36,36,256]{2,1,0:T(8,128)S(1)}, f32[36,36,256]{2,1,0:T(8,128)S(1)}) fusion(f32[38,38,256]{2,1,0:T(8,128)S(1)} %get-tuple-element.31, f32[36,36]{1,0:T(8,128)S(1)} %broadcast_multiply_fusion.1, f32[38,38,256]{2,1,0:T(8,128)S(1)} %copy-done.14, f32[38,38,256]{2,1,0:T(8,128)S(1)} %copy-done.11, f32[38,38,256]{2,1,0:T(8,128)S(1)} %copy-done.8, ...), kind=kLoop, calls=%fused_computation.135 | loop fusion | flops 6635520 | bytes 23400448 | tf_op jit(solution)/shard_map/add | solution.py:116
  196.1 4.5 %fusion.56 = f32[34,34,256]{2,1,0:T(8,128)} fusion(f32[36,36,256]{2,1,0:T(8,128)S(1)} %get-tuple-element.13, f32[36,36,256]{2,1,0:T(8,128)S(1)} %get-tuple-element.12, f32[38,38,256]{2,1,0:T(8,128)S(1)} %get-tuple-element.30, f32[38,38,256]{2,1,0:T(8,128)S(1)} %copy-done.14, f32[38,38,256]{2,1,0:T(8,128)S(1)} %copy-done.11, ...), kind=kLoop, calls=%fused_computation.112 | loop fusion | flops 5918720 | bytes 22175744 | tf_op jit(solution)/shard_map/add | solution.py:122
  200.6 8.5 %fusion.85 = f32[32,32,256]{2,1,0:T(8,128)} fusion(f32[32,32,256]{2,1,0:T(8,128)} %copy-done.20, f32[34,34,256]{2,1,0:T(8,128)} %fusion.56, f32[32,32,256]{2,1,0:T(8,128)} %get-tuple-element.15, f32[38,38,256]{2,1,0:T(8,128)S(1)} %copy-done.14, f32[38,38,256]{2,1,0:T(8,128)S(1)} %copy-done.11, f32[38,38,256]{2,1,0:T(8,128)S(1)} %copy-done.8, ...), kind=kLoop, calls=%fused_computation.154 | loop fusion | flops 4456448 | bytes 17121288 | tf_op jit(solution)/shard_map/sub | solution.py:155
  209.1 4.3 %multiply_subtract_fusion = (f32[32,32,256]{2,1,0:T(8,128)}, f32[32,32,256]{2,1,0:T(8,128)}) fusion(f32[32,32,256]{2,1,0:T(8,128)} %get-tuple-element.16, f32[34,34,256]{2,1,0:T(8,128)} %fusion.56, f32[34,34,256]{2,1,0:T(8,128)} %copy-done.17, f32[]{:T(128)S(6)} %div.70, f32[]{:T(128)S(6)} %div.72, f32[34,34,256]{2,1,0:T(8,128)} %copy-done.15, f32[]{:T(128)S(6)} %div.66), kind=kLoop, calls=%fused_computation.177 | loop fusion | flops 2359296 | bytes 6291468 | tf_op jit(solution)/shard_map/sub | solution.py:154
  (95 shorter events, 28.8 us)
Async XLA Ops:
  0.6 14.6 %copy-start.22 = (f32[32,32,256]{2,1,0:T(8,128)S(1)}, f32[32,32,256]{2,1,0:T(8,128)}, u32[]{:S(2)}) copy-start(f32[32,32,256]{2,1,0:T(8,128)} %param.3) | copy-start | bytes 3145732
  1.7 13.6 %collective-permute-start.1 = (f32[3,32,256]{2,1,0:T(8,128)S(1)}, f32[3,32,256]{2,1,0:T(8,128)S(1)}, u32[]{:S(2)}, u32[]{:S(2)}) collective-permute-start(f32[3,32,256]{2,1,0:T(8,128)S(1)} %get-tuple-element.51), channel_id=1, source_target_pairs={{8,0},{16,8},{24,16},{9,1},{17,9},{25,17},{10,2},{18,10},{26,18},{... | collective-permute-start | bytes 294920 | tf_op jit(solution)/shard_map/ppermute | solution.py:30
  3.0 12.2 %collective-permute-start = (f32[3,32,256]{2,1,0:T(8,128)S(1)}, f32[3,32,256]{2,1,0:T(8,128)S(1)}, u32[]{:S(2)}, u32[]{:S(2)}) collective-permute-start(f32[3,32,256]{2,1,0:T(8,128)S(1)} %get-tuple-element.52), channel_id=1, source_target_pairs={{0,8},{8,16},{16,24},{1,9},{9,17},{17,25},{2,10},{10,18},{18,26},{... | collective-permute-start | bytes 294920 | tf_op jit(solution)/shard_map/ppermute | solution.py:27
  7.0 8.3 %copy-start.24 = (s32[32,32,256]{2,1,0:T(8,128)S(1)}, s32[32,32,256]{2,1,0:T(8,128)}, u32[]{:S(2)}) copy-start(s32[32,32,256]{2,1,0:T(8,128)} %param.4) | copy-start | bytes 3145732
  7.0 8.4 %collective-permute-start.5 = (s32[4,32,256]{2,1,0:T(8,128)S(1)}, s32[4,32,256]{2,1,0:T(8,128)S(1)}, u32[]{:S(2)}, u32[]{:S(2)}) collective-permute-start(s32[4,32,256]{2,1,0:T(8,128)S(1)} %get-tuple-element.49), channel_id=1, source_target_pairs={{8,0},{16,8},{24,16},{9,1},{17,9},{25,17},{10,2},{18,10},{26,18},{... | collective-permute-start | bytes 393224 | tf_op jit(solution)/shard_map/ppermute | solution.py:30
  8.5 6.9 %collective-permute-start.4 = (s32[4,32,256]{2,1,0:T(8,128)S(1)}, s32[4,32,256]{2,1,0:T(8,128)S(1)}, u32[]{:S(2)}, u32[]{:S(2)}) collective-permute-start(s32[4,32,256]{2,1,0:T(8,128)S(1)} %get-tuple-element.50), channel_id=1, source_target_pairs={{0,8},{8,16},{16,24},{1,9},{9,17},{17,25},{2,10},{10,18},{18,26},{... | collective-permute-start | bytes 393224 | tf_op jit(solution)/shard_map/ppermute | solution.py:27
  15.5 10.6 %collective-permute-start.6 = (s32[40,4,256]{2,1,0:T(4,128)S(1)}, s32[40,4,256]{2,1,0:T(4,128)S(1)}, u32[]{:S(2)}, u32[]{:S(2)}) collective-permute-start(s32[40,4,256]{2,1,0:T(4,128)S(1)} %get-tuple-element.35), channel_id=1, source_target_pairs={{0,1},{1,2},{2,3},{3,4},{4,5},{5,6},{6,7},{8,9},{9,10},{10,11},{11... | collective-permute-start | bytes 491528 | tf_op jit(solution)/shard_map/ppermute | solution.py:27
  19.0 8.3 %collective-permute-start.7 = (s32[40,4,256]{2,1,0:T(4,128)S(1)}, s32[40,4,256]{2,1,0:T(4,128)S(1)}, u32[]{:S(2)}, u32[]{:S(2)}) collective-permute-start(s32[40,4,256]{2,1,0:T(4,128)S(1)} %get-tuple-element.36), channel_id=1, source_target_pairs={{1,0},{2,1},{3,2},{4,3},{5,4},{6,5},{7,6},{9,8},{10,9},{11,10},{12... | collective-permute-start | bytes 491528 | tf_op jit(solution)/shard_map/ppermute | solution.py:30
  20.3 10.9 %collective-permute-start.2 = (f32[38,3,256]{2,1,0:T(4,128)S(1)}, f32[38,3,256]{2,1,0:T(4,128)S(1)}, u32[]{:S(2)}, u32[]{:S(2)}) collective-permute-start(f32[38,3,256]{2,1,0:T(4,128)S(1)} %get-tuple-element.41), channel_id=1, source_target_pairs={{0,1},{1,2},{2,3},{3,4},{4,5},{5,6},{6,7},{8,9},{9,10},{10,11},{11... | collective-permute-start | bytes 350216 | tf_op jit(solution)/shard_map/ppermute | solution.py:27
  24.9 8.9 %collective-permute-start.3 = (f32[38,3,256]{2,1,0:T(4,128)S(1)}, f32[38,3,256]{2,1,0:T(4,128)S(1)}, u32[]{:S(2)}, u32[]{:S(2)}) collective-permute-start(f32[38,3,256]{2,1,0:T(4,128)S(1)} %get-tuple-element.42), channel_id=1, source_target_pairs={{1,0},{2,1},{3,2},{4,3},{5,4},{6,5},{7,6},{9,8},{10,9},{11,10},{12... | collective-permute-start | bytes 350216 | tf_op jit(solution)/shard_map/ppermute | solution.py:30
  37.2 7.1 %copy-start = (f32[38,38,256]{2,1,0:T(8,128)}, f32[38,38,256]{2,1,0:T(8,128)S(1)}, u32[]{:S(2)}) copy-start(f32[38,38,256]{2,1,0:T(8,128)S(1)} %get-tuple-element.25) | copy-start | bytes 4435972
  37.2 7.1 %copy-start.3 = (f32[38,38,256]{2,1,0:T(8,128)}, f32[38,38,256]{2,1,0:T(8,128)S(1)}, u32[]{:S(2)}) copy-start(f32[38,38,256]{2,1,0:T(8,128)S(1)} %get-tuple-element.26) | copy-start | bytes 4435972
  37.2 7.1 %copy-start.6 = (f32[38,38,256]{2,1,0:T(8,128)}, f32[38,38,256]{2,1,0:T(8,128)S(1)}, u32[]{:S(2)}) copy-start(f32[38,38,256]{2,1,0:T(8,128)S(1)} %get-tuple-element.27) | copy-start | bytes 4435972
  37.2 7.1 %copy-start.9 = (f32[38,38,256]{2,1,0:T(8,128)}, f32[38,38,256]{2,1,0:T(8,128)S(1)}, u32[]{:S(2)}) copy-start(f32[38,38,256]{2,1,0:T(8,128)S(1)} %get-tuple-element.28) | copy-start | bytes 4435972
  37.2 7.1 %copy-start.12 = (f32[38,38,256]{2,1,0:T(8,128)}, f32[38,38,256]{2,1,0:T(8,128)S(1)}, u32[]{:S(2)}) copy-start(f32[38,38,256]{2,1,0:T(8,128)S(1)} %get-tuple-element.29) | copy-start | bytes 4435972
  50.2 3.3 %collective-permute-start.8 = (f32[3,32,256]{2,1,0:T(8,128)S(1)}, f32[3,32,256]{2,1,0:T(8,128)S(1)}, u32[]{:S(2)}, u32[]{:S(2)}) collective-permute-start(f32[3,32,256]{2,1,0:T(8,128)S(1)} %get-tuple-element.47), channel_id=1, source_target_pairs={{0,8},{8,16},{16,24},{1,9},{9,17},{17,25},{2,10},{10,18},{18,26},{... | collective-permute-start | bytes 294920 | tf_op jit(solution)/shard_map/ppermute | solution.py:27
  52.2 5.6 %collective-permute-start.9 = (f32[3,32,256]{2,1,0:T(8,128)S(1)}, f32[3,32,256]{2,1,0:T(8,128)S(1)}, u32[]{:S(2)}, u32[]{:S(2)}) collective-permute-start(f32[3,32,256]{2,1,0:T(8,128)S(1)} %get-tuple-element.48), channel_id=1, source_target_pairs={{8,0},{16,8},{24,16},{9,1},{17,9},{25,17},{10,2},{18,10},{26,18},{... | collective-permute-start | bytes 294920 | tf_op jit(solution)/shard_map/ppermute | solution.py:30
  59.6 51.2 %collective-permute-start.10 = (f32[38,3,256]{2,1,0:T(4,128)}, f32[38,3,256]{2,1,0:T(4,128)S(1)}, u32[]{:S(2)}, u32[]{:S(2)}) collective-permute-start(f32[38,3,256]{2,1,0:T(4,128)} %get-tuple-element.39), channel_id=1, source_target_pairs={{0,1},{1,2},{2,3},{3,4},{4,5},{5,6},{6,7},{8,9},{9,10},{10,11},{11... | collective-permute-start | bytes 350216 | tf_op jit(solution)/shard_map/ppermute | solution.py:27
  64.4 46.4 %collective-permute-start.11 = (f32[38,3,256]{2,1,0:T(4,128)}, f32[38,3,256]{2,1,0:T(4,128)}, u32[]{:S(2)}, u32[]{:S(2)}) collective-permute-start(f32[38,3,256]{2,1,0:T(4,128)} %get-tuple-element.40), channel_id=1, source_target_pairs={{1,0},{2,1},{3,2},{4,3},{5,4},{6,5},{7,6},{9,8},{10,9},{11,10},{12... | collective-permute-start | bytes 350216 | tf_op jit(solution)/shard_map/ppermute | solution.py:30
  127.6 51.9 %collective-permute-start.12 = (f32[3,32,256]{2,1,0:T(8,128)S(1)}, f32[3,32,256]{2,1,0:T(8,128)S(1)}, u32[]{:S(2)}, u32[]{:S(2)}) collective-permute-start(f32[3,32,256]{2,1,0:T(8,128)S(1)} %get-tuple-element.45), channel_id=1, source_target_pairs={{0,8},{8,16},{16,24},{1,9},{9,17},{17,25},{2,10},{10,18},{18,26},{... | collective-permute-start | bytes 294920 | tf_op jit(solution)/shard_map/ppermute | solution.py:27
  128.9 50.6 %collective-permute-start.13 = (f32[3,32,256]{2,1,0:T(8,128)S(1)}, f32[3,32,256]{2,1,0:T(8,128)S(1)}, u32[]{:S(2)}, u32[]{:S(2)}) collective-permute-start(f32[3,32,256]{2,1,0:T(8,128)S(1)} %get-tuple-element.46), channel_id=1, source_target_pairs={{8,0},{16,8},{24,16},{9,1},{17,9},{25,17},{10,2},{18,10},{26,18},{... | collective-permute-start | bytes 294920 | tf_op jit(solution)/shard_map/ppermute | solution.py:30
  180.7 10.3 %collective-permute-start.14 = (f32[38,3,256]{2,1,0:T(4,128)S(1)}, f32[38,3,256]{2,1,0:T(4,128)S(1)}, u32[]{:S(2)}, u32[]{:S(2)}) collective-permute-start(f32[38,3,256]{2,1,0:T(4,128)S(1)} %get-tuple-element.37), channel_id=1, source_target_pairs={{0,1},{1,2},{2,3},{3,4},{4,5},{5,6},{6,7},{8,9},{9,10},{10,11},{11... | collective-permute-start | bytes 350216 | tf_op jit(solution)/shard_map/ppermute | solution.py:27
  184.9 7.3 %copy-start.21 = (f32[32,32,256]{2,1,0:T(8,128)S(1)}, f32[32,32,256]{2,1,0:T(8,128)}, u32[]{:S(2)}) copy-start(f32[32,32,256]{2,1,0:T(8,128)} %copy-done.20) | copy-start | bytes 3145732
  184.9 7.3 %collective-permute-start.15 = (f32[38,3,256]{2,1,0:T(4,128)S(1)}, f32[38,3,256]{2,1,0:T(4,128)S(1)}, u32[]{:S(2)}, u32[]{:S(2)}) collective-permute-start(f32[38,3,256]{2,1,0:T(4,128)S(1)} %get-tuple-element.38), channel_id=1, source_target_pairs={{1,0},{2,1},{3,2},{4,3},{5,4},{6,5},{7,6},{9,8},{10,9},{11,10},{12... | collective-permute-start | bytes 350216 | tf_op jit(solution)/shard_map/ppermute | solution.py:30
  (17 other events, 60.6 us)
where the time goes:
time: 214 us; the launch traced here: 213 us
  blocking collectives  88.7 us (41%)
  other arithmetic  60.4 us (28%)
  starting transfers between devices  39.3 us (18%)
  waiting for transfers between devices  11 us (5%)
  local copies, waits for them, and re-layouts  7.11 us (3%)
  between operations  6.88 us (3%)
    psum x2, blocking collectives, local(): lax.psum((jnp.sum(residual * pre_residual), jnp.sum(residual_image * pre_...  88.7 us
    ppermute x8, starting transfers between devices, extended_2(): lax.ppermute(lax.slice_in_dim(block, block.shape[dim] - width, None, axis...  28.4 us
    add x3, other arithmetic, composite(): second = shrink(first, 1) + change  12 us
    add x3, other arithmetic, composite(): third = shrink(second, 1) + change  11.4 us
    ppermute x8, starting transfers between devices, extended_2(): lax.ppermute(lax.slice_in_dim(block, 0, width, axis=dim), axis, backward)  10.8 us
    ppermute x8, waiting for transfers between devices, extended_2(): lax.ppermute(lax.slice_in_dim(block, 0, width, axis=dim), axis, backward)  9.17 us
    reduce_sum x2, other arithmetic, local(): jnp.sum(residual_image * pre_residual)  9.03 us
    sub x1, other arithmetic, local(): residual_image = residual_image - step_size * image_dir  8.48 us
  transfers between devices with their start and end apart: 16, of which 6 were waited for; matrix products, arithmetic and copies ran while one was open for 4% of the time, Pallas kernels for 0%

commit v1 on v0

v1 whole, which is shorter than its diff:
```python
import functools

import jax
import jax.numpy as jnp
from jax import lax
from jax.experimental import pallas as pl
from jax.experimental.pallas import tpu as pltpu
from jax.sharding import PartitionSpec as P

MESH = pl.DeviceIdType.MESH

centre_value = 1.1
half_width = 0.9
ratio_sigma = centre_value / half_width
rho_first = 1.0 / ratio_sigma
rho_second = 1.0 / (2.0 * ratio_sigma - rho_first)
rho_third = 1.0 / (2.0 * ratio_sigma - rho_second)
start_scale = 1.0 / centre_value
keep_first = rho_second * rho_first
push_first = 2.0 * rho_second / half_width
keep_second = rho_third * rho_second
push_second = 2.0 * rho_third / half_width

own_first = start_scale * (1.0 + keep_first) + push_first * (1.0 - start_scale)
near_first = push_first * start_scale
own_second = 1.0 + keep_second - push_second
base_second = push_second - keep_second * start_scale

EXCHANGES = 10


def loop(low, high, body, carry=None):
    count = high - low
    unroll = next(u for u in (4, 5, 3, 2, 1) if count % u == 0)

    def step(k, value):
        for j in range(unroll):
            value = body(low + k * unroll + j, value)
        return value

    return lax.fori_loop(0, count // unroll, step, carry)


def fold(block):
    rows, lanes = block.shape
    tile = block[0:8]
    for k in range(1, rows // 8):
        tile = tile + block[8 * k : 8 * k + 8]
    out = tile[:, 0:128]
    for k in range(1, lanes // 128):
        out = out + tile[:, 128 * k : 128 * k + 128]
    return out


def total(tile):
    return jnp.sum(jnp.sum(tile, axis=0, keepdims=True), axis=1, keepdims=True)


def kernel(
    ngx, ngy,
    right_ref, phase_ref, table_ref,
    x_out, r_out, u_out, w_out,
    rho, cx, cs, cd, diag, inv,
    ys, firsts, seconds, images,
    w_next, r_next, u_next,
    pack_s, pack_n, inv_s, inv_n, side_s, side_n,
    face_x, face_y, gain_x, gain_y,
    halo_x, halo_y, red_x, red_y,
    send_sem, recv_sem, rx_send, rx_recv, ry_send, ry_recv,
):
    nx, ny, nz = right_ref.shape
    gx = lax.axis_index("gx")
    gy = lax.axis_index("gy")
    has = (gx > 0, gx < ngx - 1, gy > 0, gy < ngy - 1)

    barrier = pltpu.get_barrier_semaphore()
    for k in range(1, ngx):
        pl.semaphore_signal(barrier, inc=1, device_id={"gx": lax.rem(gx + k, ngx)}, device_id_type=MESH)
    for k in range(1, ngy):
        pl.semaphore_signal(barrier, inc=1, device_id={"gy": lax.rem(gy + k, ngy)}, device_id_type=MESH)

    def halo(e, side):
        return halo_x.at[e, side] if side < 2 else halo_y.at[e, side - 2]

    def copy_of(e, side, src):
        axis, position = ("gx", gx) if side < 2 else ("gy", gy)
        step = -1 if side % 2 == 0 else 1
        return pltpu.make_async_remote_copy(
            src_ref=src,
            dst_ref=halo(e, side ^ 1),
            send_sem=send_sem.at[e, side],
            recv_sem=recv_sem.at[e, side ^ 1],
            device_id={axis: position + step},
            device_id_type=MESH,
        )

    sent = []

    def send(e, sources):
        for side in range(4):
            pl.when(has[side])(functools.partial(lambda c: c.start(), copy_of(e, side, sources[side])))
        sent.append((e, sources))

    def arrive(e):
        for side in range(4):
            dummy = pltpu.make_async_remote_copy(
                src_ref=halo(e, side),
                dst_ref=halo(e, side),
                send_sem=send_sem.at[e, side],
                recv_sem=recv_sem.at[e, side],
                device_id={"gx": gx, "gy": gy},
                device_id_type=MESH,
            )
            pl.when(has[side])(functools.partial(lambda c: c.wait_recv(), dummy))

    t1, t2, t3 = (jnp.full((1, 1), table_ref[k], jnp.float32) for k in (1, 2, 3))
    q0 = 1.0 / jnp.full((1, 1), table_ref[0], jnp.float32)
    q1, q2, q3 = 1.0 / t1, 1.0 / t2, 1.0 / t3

    for side in range(4):
        def outside(side=side):
            for e in range(EXCHANGES):
                target = halo(e, side)
                fill = jnp.zeros(target.shape, jnp.float32)
                target[...] = fill + q0 if e == 0 else fill

        pl.when(jnp.logical_not(has[side]))(outside)

    def lookup_plane(i, _):
        labels = phase_ref[i]
        value = jnp.where(labels == 1, q1, jnp.where(labels == 2, q2, jnp.where(labels == 3, q3, q0)))
        rho[i] = value
        pack_s[0, pl.ds(i, 1), :] = value[0:1]
        pack_n[0, pl.ds(i, 1), :] = value[ny - 1 : ny]
        right = right_ref[i]
        side_s[4, pl.ds(i, 1), :] = right[0:1]
        side_n[4, pl.ds(i, 1), :] = right[ny - 1 : ny]

    loop(0, nx, lookup_plane)
    pl.semaphore_wait(barrier, ngx - 1 + ngy - 1)
    send(0, (rho.at[0], rho.at[nx - 1], pack_s.at[0], pack_n.at[0]))

    row = lax.broadcasted_iota(jnp.int32, (ny, nz), 0)
    lane = lax.broadcasted_iota(jnp.int32, (ny, nz), 1)
    zero = jnp.zeros((ny, nz), jnp.float32)
    cx[0] = zero
    cx[nx] = zero
    for c in range(3):
        for buffer in (ys, firsts, seconds):
            buffer[c, 0] = zero
            buffer[c, nx + 1] = zero

    def couple_x(i, _):
        cx[i] = 2.0 / (rho[i - 1] + rho[i])

    loop(1, nx, couple_x)

    def couple_rest(i, _):
        here = rho[i]
        south = jnp.where(row == 0, 0.0, 2.0 / (here + pltpu.roll(here, 1, 0)))
        beside = jnp.where(lane == 0, q0, pltpu.roll(here, 1, 1))
        down = 2.0 / (here + beside)
        last = 2.0 / (here[:, nz - 128 :] + q0)
        last = jnp.concatenate([jnp.zeros((ny, nz - 128), jnp.float32), last], axis=1)
        inner = jnp.where(lane == 0, 0.0, down)
        cs[i] = south
        cd[i] = inner
        up = jnp.where(lane == nz - 1, last, pltpu.roll(inner, nz - 1, 1))
        d = cx[i] + cx[i + 1] + south + pltpu.roll(south, ny - 1, 0) + down + up
        diag[i] = d
        side_s[3, pl.ds(i, 1), :] = d[0:1]
        side_n[3, pl.ds(i, 1), :] = d[ny - 1 : ny]

    loop(0, nx, couple_rest)

    def scatter(ref, first, row_s, row_n):
        def one(i, _):
            ref[first + i, 0:1, :] = row_s[pl.ds(i, 1), :]
            ref[first + i, ny - 1 : ny, :] = row_n[pl.ds(i, 1), :]

        loop(1, nx - 1, one)

    def correct(ref, first, row_s, row_n, add_x, add_y):
        edge = (first, first + nx - 1)
        for side in range(2):
            ref[edge[side]] = ref[edge[side]] + add_x(side)
        for side, i in ((0, 0), (1, nx - 1)):
            row_s[i : i + 1, :] = ref[edge[side], 0:1, :]
            row_n[i : i + 1, :] = ref[edge[side], ny - 1 : ny, :]
        row_s[...] = row_s[...] + add_y(0)
        row_n[...] = row_n[...] + add_y(1)
        for side, i in ((0, 0), (1, nx - 1)):
            ref[edge[side], 0:1, :] = row_s[i : i + 1, :]
            ref[edge[side], ny - 1 : ny, :] = row_n[i : i + 1, :]

    arrive(0)
    for side, plane in ((0, 0), (1, nx - 1)):
        face_x[side] = 2.0 / (rho[plane] + halo_x[0, side])
    face_y[0] = 2.0 / (pack_s[0] + halo_y[0, 0])
    face_y[1] = 2.0 / (pack_n[0] + halo_y[0, 1])
    ds_, dn_ = side_s.at[3], side_n.at[3]
    correct(diag, 0, ds_, dn_, lambda s: face_x[s], lambda s: face_y[s])
    inv_s[...] = 1.0 / ds_[...]
    inv_n[...] = 1.0 / dn_[...]
    for side, plane in ((0, 0), (1, nx - 1)):
        inv[plane] = 1.0 / diag[plane]
        gain_x[side] = face_x[side] * inv[plane]
    gain_y[0] = face_y[0] * inv_s[...]
    gain_y[1] = face_y[1] * inv_n[...]

    def near(f, i):
        here = f[i + 1]
        south = cs[i]
        down = cd[i]
        return (
            (cx[i] * f[i] + cx[i + 1] * f[i + 2])
            + (south * pltpu.roll(here, 1, 0) + pltpu.roll(south * here, ny - 1, 0))
            + (down * pltpu.roll(here, 1, 1) + pltpu.roll(down * here, nz - 1, 1))
        )

    def send_y(e, y, plane_value, value_s, value_n):
        for plane in (0, nx - 1):
            y[plane + 1] = plane_value(plane) * inv[plane]
        pack_s[e] = value_s * inv_s[...]
        pack_n[e] = value_n * inv_n[...]
        send(e, (y.at[1], y.at[nx], pack_s.at[e], pack_n.at[e]))

    def gained(scale, e):
        return (
            lambda s: (scale * gain_x[s]) * halo_x[e, s],
            lambda s: (scale * gain_y[s]) * halo_y[e, s],
        )

    def composite(c, e, between):
        y, first, second, image = ys.at[c], firsts.at[c], seconds.at[c], images.at[c]

        def step_first(i, _):
            value = own_first * y[i + 1] + near_first * (inv[i] * near(y, i))
            first[i + 1] = value
            pack_s[e + 1, pl.ds(i, 1), :] = value[0:1]
            pack_n[e + 1, pl.ds(i, 1), :] = value[ny - 1 : ny]

        loop(0, nx, step_first)
        arrive(e)
        row_s, row_n = pack_s.at[e + 1], pack_n.at[e + 1]
        correct(first, 1, row_s, row_n, *gained(near_first, e))
        send(e + 1, (first.at[1], first.at[nx], row_s, row_n))
        scatter(first, 1, row_s, row_n)
        between(0)

        def step_second(i, _):
            value = own_second * first[i + 1] + base_second * y[i + 1] + push_second * (inv[i] * near(first, i))
            second[i + 1] = value
            pack_s[e + 2, pl.ds(i, 1), :] = value[0:1]
            pack_n[e + 2, pl.ds(i, 1), :] = value[ny - 1 : ny]

        loop(0, nx, step_second)
        arrive(e + 1)
        row_s2, row_n2 = pack_s.at[e + 2], pack_n.at[e + 2]
        correct(second, 1, row_s2, row_n2, *gained(push_second, e + 1))
        send(e + 2, (second.at[1], second.at[nx], row_s2, row_n2))
        scatter(second, 1, row_s2, row_n2)
        between(1)

        def step_image(i, _):
            value = diag[i] * second[i + 1] - near(second, i)
            image[i] = value
            side_s[c, pl.ds(i, 1), :] = value[0:1]
            side_n[c, pl.ds(i, 1), :] = value[ny - 1 : ny]

        loop(0, nx, step_image)
        arrive(e + 2)
        correct(
            image, 0, side_s.at[c], side_n.at[c],
            lambda s: -(face_x[s] * halo_x[e + 2, s]),
            lambda s: -(face_y[s] * halo_y[e + 2, s]),
        )

    def reduce_start(buffer, axis, position, count, send_sems, recv_sems):
        for k in range(1, count):
            reduce_copy(buffer, axis, position, count, k, send_sems, recv_sems).start()

    def reduce_copy(buffer, axis, position, count, k, send_sems, recv_sems):
        return pltpu.make_async_remote_copy(
            src_ref=buffer.at[0],
            dst_ref=buffer.at[k],
            send_sem=send_sems.at[k],
            recv_sem=recv_sems.at[k],
            device_id={axis: lax.rem(position + k, count)},
            device_id_type=MESH,
        )

    def reduce_end(buffer, axis, position, count, send_sems, recv_sems):
        value = buffer[0]
        for k in range(1, count):
            reduce_copy(buffer, axis, position, count, k, send_sems, recv_sems).wait()
            value = value + buffer[k]
        return value

    def over_x(t):
        return red_x.at[t], "gx", gx, ngx, rx_send.at[t], rx_recv.at[t]

    def over_y(t):
        return red_y.at[t], "gy", gy, ngy, ry_send.at[t], ry_recv.at[t]

    def put_sums(t, sums):
        red_x[t, 0, 0:8, :] = sums[0]
        red_x[t, 0, 8:16, :] = sums[1]
        reduce_start(*over_x(t))

    def relay(t):
        red_y[t, 0] = reduce_end(*over_x(t))
        reduce_start(*over_y(t))

    def take_sums(t):
        both = reduce_end(*over_y(t))
        return total(both[0:8]), total(both[8:16])

    send_y(1, ys.at[0], lambda p: right_ref[p], side_s[4], side_n[4])
    scatter(diag, 0, ds_, dn_)

    def start_plane(i, _):
        value = 1.0 / diag[i]
        inv[i] = value
        ys[0, i + 1] = right_ref[i] * value

    loop(1, nx - 1, start_plane)
    composite(0, 1, lambda k: None)

    w0, u0 = images.at[0], seconds.at[0]
    send_y(4, ys.at[1], lambda p: w0[p], side_s[0], side_n[0])
    scatter(w0, 0, side_s.at[0], side_n.at[0])
    tile = jnp.zeros((8, 128), jnp.float32)

    def second_plane(i, sums):
        w = w0[i]
        u = u0[i + 1]
        ys[1, i + 1] = w * inv[i]
        return sums[0] + fold(right_ref[i] * u), sums[1] + fold(w * u)

    sums = (tile, tile)
    for plane in (0, nx - 1):
        u = u0[plane + 1]
        sums = (sums[0] + fold(right_ref[plane] * u), sums[1] + fold(w0[plane] * u))
    put_sums(0, loop(1, nx - 1, second_plane, sums))
    composite(1, 4, lambda k: relay(0) if k == 0 else None)
    g0, h0 = take_sums(0)
    a0 = g0 / h0

    m0, n0 = seconds.at[1], images.at[1]
    for plane in (0, nx - 1):
        w_next[plane] = w0[plane] - a0 * n0[plane]
    send_y(7, ys.at[2], lambda p: w_next[p], side_s[0] - a0 * side_s[1], side_n[0] - a0 * side_n[1])
    scatter(n0, 0, side_s.at[1], side_n.at[1])

    def advance(i, sums):
        w = w_next[i]
        r = right_ref[i] - a0 * w0[i]
        u = u0[i + 1] - a0 * m0[i + 1]
        r_next[i] = r
        u_next[i] = u
        return sums[0] + fold(r * u), sums[1] + fold(w * u)

    def third_plane(i, sums):
        w = w0[i] - a0 * n0[i]
        w_next[i] = w
        ys[2, i + 1] = w * inv[i]
        return advance(i, sums)

    sums = (tile, tile)
    for plane in (0, nx - 1):
        sums = advance(plane, sums)
    put_sums(1, loop(1, nx - 1, third_plane, sums))
    composite(2, 7, lambda k: relay(1) if k == 0 else None)
    scatter(images.at[2], 0, side_s.at[2], side_n.at[2])
    g1, h1 = take_sums(1)
    b = g1 / g0
    a1 = g1 / (h1 - b * g1 / a0)

    def finish(i, _):
        u = u_next[i]
        x_out[i] = a0 * u0[i + 1] + a1 * (u + b * u0[i + 1])
        r_out[i] = r_next[i] - a1 * (w_next[i] + b * w0[i])
        u_out[i] = u - a1 * (seconds[2, i + 1] + b * m0[i + 1])
        w_out[i] = w_next[i] - a1 * (images[2, i] + b * n0[i])

    loop(0, nx, finish)

    for e, sources in sent:
        for side in range(4):
            pl.when(has[side])(functools.partial(lambda c: c.wait_send(), copy_of(e, side, sources[side])))


def solution(mesh):
    ngx, ngy = mesh.shape["gx"], mesh.shape["gy"]

    def local(right_side, phase, table):
        nx, ny, nz = right_side.shape
        f32 = jnp.float32
        block = pltpu.VMEM((nx, ny, nz), f32)
        three = pltpu.VMEM((3, nx + 2, ny, nz), f32)
        packed = pltpu.VMEM((EXCHANGES, nx, nz), f32)
        packed_one = pltpu.VMEM((nx, nz), f32)
        sides = pltpu.VMEM((5, nx, nz), f32)
        whole = pl.BlockSpec(memory_space=pltpu.VMEM)
        return pl.pallas_call(
            functools.partial(kernel, ngx, ngy),
            out_shape=[jax.ShapeDtypeStruct((nx, ny, nz), f32)] * 4,
            in_specs=[whole, whole, pl.BlockSpec(memory_space=pltpu.SMEM)],
            out_specs=[whole] * 4,
            scratch_shapes=[
                block, pltpu.VMEM((nx + 1, ny, nz), f32), block, block, block, block,
                three, three, three, pltpu.VMEM((3, nx, ny, nz), f32),
                block, block, block,
                packed, packed, packed_one, packed_one, sides, sides,
                pltpu.VMEM((2, ny, nz), f32), pltpu.VMEM((2, nx, nz), f32),
                pltpu.VMEM((2, ny, nz), f32), pltpu.VMEM((2, nx, nz), f32),
                pltpu.VMEM((EXCHANGES, 2, ny, nz), f32), pltpu.VMEM((EXCHANGES, 2, nx, nz), f32),
                pltpu.VMEM((2, ngx, 16, 128), f32), pltpu.VMEM((2, ngy, 16, 128), f32),
                pltpu.SemaphoreType.DMA((EXCHANGES, 4)), pltpu.SemaphoreType.DMA((EXCHANGES, 4)),
                pltpu.SemaphoreType.DMA((2, ngx)), pltpu.SemaphoreType.DMA((2, ngx)),
                pltpu.SemaphoreType.DMA((2, ngy)), pltpu.SemaphoreType.DMA((2, ngy)),
            ],
            compiler_params=pltpu.CompilerParams(
                collective_id=0, has_side_effects=True, vmem_limit_bytes=56 * 1024 * 1024
            ),
        )(right_side, phase, table)

    spec = P("gx", "gy", None)
    return jax.shard_map(
        local, mesh=mesh, in_specs=(spec, spec, P()), out_specs=(spec,) * 4, check_vma=False
    )
```

time: 214 us -> 54 us (0.25)
  blocking collectives: 88.7 us -> 0 us
  other arithmetic: 60.4 us -> 0 us
  Pallas kernels: 0 us -> 45.9 us
  starting transfers between devices: 39.3 us -> 0 us
  waiting for transfers between devices: 11 us -> 0 us
  between operations: 6.88 us -> 0.65 us
    psum x2 -> x0, blocking collectives: 88.7 us -> none  [local(): lax.psum((jnp.sum(residual * pre_residual), jnp.sum(residual_image * pre_...]
    pallas_call x0 -> x1, Pallas kernels: none -> 45.9 us  [local(): pl.pallas_call(functools.partial(kernel, ngx, ngy), out_shape=[jax.ShapeD...]
    ppermute x16 -> x0, starting transfers between devices: 39.3 us -> none  [the longest x8 28.4 us: extended_2(): lax.ppermute(lax.slice_in_dim(block, block.shape[dim] - width, None, axis...]
    add x6 -> x0, other arithmetic: 23.5 us -> none  [the longest x3 12 us: composite(): second = shrink(first, 1) + change]
    sub x3 -> x0, other arithmetic: 15.8 us -> none  [the longest x1 8.48 us: local(): residual_image = residual_image - step_size * image_dir]
    ppermute x16 -> x0, waiting for transfers between devices: 11 us -> none  [the longest x8 9.17 us: extended_2(): lax.ppermute(lax.slice_in_dim(block, 0, width, axis=dim), axis, backward)]
    reduce_sum x2 -> x0, other arithmetic: 9.03 us -> none  [local(): jnp.sum(residual_image * pre_residual)]
    slice x7 -> x0, local copies, waits for them, and re-layouts: 4.52 us -> none  [the longest x2 2.03 us: extended_2(): lax.slice_in_dim(block, 0, width, axis=dim)]
  transfers between devices with their start and end apart: 16 -> 0, of which waited for: 6 -> 0; matrix products, arithmetic and copies ran while one was open for 4% -> 0% of each run, Pallas kernels for 0% -> 0%
where the time goes in v1:
time: 54 us; the launch traced here: 53.2 us
  Pallas kernels  45.9 us (85%)
  local copies, waits for them, and re-layouts  6.57 us (12%)
  between operations  0.65 us (1%)
    pallas_call x1, Pallas kernels, local(): pl.pallas_call(functools.partial(kernel, ngx, ngy), out_shape=[jax.ShapeD...  45.9 us
    unnamed x10, local copies, waits for them, and re-layouts  6.57 us

profile of v1, /device:TPU:0, one launch (start us, length us, event | category | flops | bytes accessed | tf_op | source)
XLA Modules:
  0.0 53.2 jit_solution(1721939825483536329)
XLA Ops:
  0.6 45.9 %shard_map.66 = (f32[32,32,256]{2,1,0:T(8,128)}, f32[32,32,256]{2,1,0:T(8,128)}, f32[32,32,256]{2,1,0:T(8,128)}, f32[32,32,256]{2,1,0:T(8,128)}) custom-call(f32[32,32,256]{2,1,0:T(8,128)} %right_ref.1, s32[32,32,256]{2,1,0:T(8,128)} %phase_ref.1, f32[4]{0:T(128)} %table_ref.1), custom_call_target="tpu_custom_call" | custom-call | tf_op jit(solution)/shard_map/pallas_call | solution.py:406
  46.6 0.0 copy-start.2
  46.6 2.4 %copy.11 = f32[32,32,256]{2,1,0:T(8,128)} copy(f32[32,32,256]{2,1,0:T(8,128)} %get-tuple-element.8) | data formatting | bytes 2097152
  49.0 0.0 copy-done.2
  49.0 0.0 copy-start.1
  49.0 1.0 %copy.12 = f32[32,32,256]{2,1,0:T(8,128)} copy(f32[32,32,256]{2,1,0:T(8,128)S(1)} %copy-done.2) | data formatting | bytes 2097152
  50.0 0.6 %copy-done.1 = f32[32,32,256]{2,1,0:T(8,128)S(1)} copy-done((f32[32,32,256]{2,1,0:T(8,128)S(1)}, f32[32,32,256]{2,1,0:T(8,128)}, u32[]{:S(2)}) %copy-start.1) | copy-done | bytes 1048600
  50.6 0.0 copy-start
  50.6 1.0 %copy.13 = f32[32,32,256]{2,1,0:T(8,128)} copy(f32[32,32,256]{2,1,0:T(8,128)S(1)} %copy-done.1) | data formatting | bytes 2097152
  51.6 0.6 %copy-done = f32[32,32,256]{2,1,0:T(8,128)S(1)} copy-done((f32[32,32,256]{2,1,0:T(8,128)S(1)}, f32[32,32,256]{2,1,0:T(8,128)}, u32[]{:S(2)}) %copy-start) | copy-done | bytes 1048600
  52.2 1.0 %copy.14 = f32[32,32,256]{2,1,0:T(8,128)} copy(f32[32,32,256]{2,1,0:T(8,128)S(1)} %copy-done) | data formatting | bytes 2097152
Async XLA Ops:
  46.6 2.4 %copy-start.2 = (f32[32,32,256]{2,1,0:T(8,128)S(1)}, f32[32,32,256]{2,1,0:T(8,128)}, u32[]{:S(2)}) copy-start(f32[32,32,256]{2,1,0:T(8,128)} %get-tuple-element.9) | copy-start | bytes 3145732
  49.0 1.6 %copy-start.1 = (f32[32,32,256]{2,1,0:T(8,128)S(1)}, f32[32,32,256]{2,1,0:T(8,128)}, u32[]{:S(2)}) copy-start(f32[32,32,256]{2,1,0:T(8,128)} %get-tuple-element.10) | copy-start | bytes 3145732
  50.6 1.6 %copy-start = (f32[32,32,256]{2,1,0:T(8,128)S(1)}, f32[32,32,256]{2,1,0:T(8,128)}, u32[]{:S(2)}) copy-start(f32[32,32,256]{2,1,0:T(8,128)} %get-tuple-element.11) | copy-start | bytes 3145732

commit v2 on v1

--- a/solution.py
+++ b/solution.py
@@ -59,10 +59,9 @@
 def kernel(
     ngx, ngy,
     right_ref, phase_ref, table_ref,
-    x_out, r_out, u_out, w_out,
+    seconds, images, steps,
     rho, cx, cs, cd, diag, inv,
-    ys, firsts, seconds, images,
-    w_next, r_next, u_next,
+    ys, firsts, w_next,
     pack_s, pack_n, inv_s, inv_n, side_s, side_n,
     face_x, face_y, gain_x, gain_y,
     halo_x, halo_y, red_x, red_y,
@@ -96,13 +95,12 @@
 
     sent = []
 
-    def send(e, sources):
-        for side in range(4):
-            pl.when(has[side])(functools.partial(lambda c: c.start(), copy_of(e, side, sources[side])))
-        sent.append((e, sources))
-
-    def arrive(e):
-        for side in range(4):
+    def send(e, side, source):
+        pl.when(has[side])(functools.partial(lambda c: c.start(), copy_of(e, side, source)))
+        sent.append((e, side, source))
+
+    def arrive(e, sides):
+        for side in sides:
             dummy = pltpu.make_async_remote_copy(
                 src_ref=halo(e, side),
                 dst_ref=halo(e, side),
@@ -138,7 +136,10 @@
 
     loop(0, nx, lookup_plane)
     pl.semaphore_wait(barrier, ngx - 1 + ngy - 1)
-    send(0, (rho.at[0], rho.at[nx - 1], pack_s.at[0], pack_n.at[0]))
+    send(0, 2, pack_s.at[0])
+    send(0, 3, pack_n.at[0])
+    send(0, 0, rho.at[0])
+    send(0, 1, rho.at[nx - 1])
 
     row = lax.broadcasted_iota(jnp.int32, (ny, nz), 0)
     lane = lax.broadcasted_iota(jnp.int32, (ny, nz), 1)
@@ -180,26 +181,41 @@
 
         loop(1, nx - 1, one)
 
-    def correct(ref, first, row_s, row_n, add_x, add_y):
+    def settle(e, ref, first, row_s, row_n, add_x, add_y, e_out=None):
         edge = (first, first + nx - 1)
-        for side in range(2):
-            ref[edge[side]] = ref[edge[side]] + add_x(side)
+        arrive(e, (0, 1))
         for side, i in ((0, 0), (1, nx - 1)):
-            row_s[i : i + 1, :] = ref[edge[side], 0:1, :]
-            row_n[i : i + 1, :] = ref[edge[side], ny - 1 : ny, :]
-        row_s[...] = row_s[...] + add_y(0)
-        row_n[...] = row_n[...] + add_y(1)
+            plane = ref[edge[side]] + add_x(side)
+            ref[edge[side]] = plane
+            row_s[i : i + 1, :] = plane[0:1]
+            row_n[i : i + 1, :] = plane[ny - 1 : ny]
+        for k, rows in ((0, row_s), (1, row_n)):
+            arrive(e, (2 + k,))
+            rows[...] = rows[...] + add_y(k)
+            if e_out is not None:
+                send(e_out, 2 + k, rows)
         for side, i in ((0, 0), (1, nx - 1)):
             ref[edge[side], 0:1, :] = row_s[i : i + 1, :]
             ref[edge[side], ny - 1 : ny, :] = row_n[i : i + 1, :]
-
-    arrive(0)
+            if e_out is not None:
+                send(e_out, side, ref.at[edge[side]])
+
+    arrive(0, range(4))
     for side, plane in ((0, 0), (1, nx - 1)):
         face_x[side] = 2.0 / (rho[plane] + halo_x[0, side])
     face_y[0] = 2.0 / (pack_s[0] + halo_y[0, 0])
     face_y[1] = 2.0 / (pack_n[0] + halo_y[0, 1])
     ds_, dn_ = side_s.at[3], side_n.at[3]
-    correct(diag, 0, ds_, dn_, lambda s: face_x[s], lambda s: face_y[s])
+    for side, plane in ((0, 0), (1, nx - 1)):
+        whole = diag[plane] + face_x[side]
+        diag[plane] = whole
+        ds_[plane : plane + 1, :] = whole[0:1]
+        dn_[plane : plane + 1, :] = whole[ny - 1 : ny]
+    ds_[...] = ds_[...] + face_y[0]
+    dn_[...] = dn_[...] + face_y[1]
+    for plane in (0, nx - 1):
+        diag[plane, 0:1, :] = ds_[plane : plane + 1, :]
+        diag[plane, ny - 1 : ny, :] = dn_[plane : plane + 1, :]
     inv_s[...] = 1.0 / ds_[...]
     inv_n[...] = 1.0 / dn_[...]
     for side, plane in ((0, 0), (1, nx - 1)):
@@ -219,11 +235,13 @@
         )
 
     def send_y(e, y, plane_value, value_s, value_n):
-        for plane in (0, nx - 1):
+        pack_s[e] = value_s * inv_s[...]
+        send(e, 2, pack_s.at[e])
+        pack_n[e] = value_n * inv_n[...]
+        send(e, 3, pack_n.at[e])
+        for side, plane in ((0, 0), (1, nx - 1)):
             y[plane + 1] = plane_value(plane) * inv[plane]
-        pack_s[e] = value_s * inv_s[...]
-        pack_n[e] = value_n * inv_n[...]
-        send(e, (y.at[1], y.at[nx], pack_s.at[e], pack_n.at[e]))
+            send(e, side, y.at[plane + 1])
 
     def gained(scale, e):
         return (
@@ -241,10 +259,8 @@
             pack_n[e + 1, pl.ds(i, 1), :] = value[ny - 1 : ny]
 
         loop(0, nx, step_first)
-        arrive(e)
         row_s, row_n = pack_s.at[e + 1], pack_n.at[e + 1]
-        correct(first, 1, row_s, row_n, *gained(near_first, e))
-        send(e + 1, (first.at[1], first.at[nx], row_s, row_n))
+        settle(e, first, 1, row_s, row_n, *gained(near_first, e), e + 1)
         scatter(first, 1, row_s, row_n)
         between(0)
 
@@ -255,10 +271,8 @@
             pack_n[e + 2, pl.ds(i, 1), :] = value[ny - 1 : ny]
 
         loop(0, nx, step_second)
-        arrive(e + 1)
         row_s2, row_n2 = pack_s.at[e + 2], pack_n.at[e + 2]
-        correct(second, 1, row_s2, row_n2, *gained(push_second, e + 1))
-        send(e + 2, (second.at[1], second.at[nx], row_s2, row_n2))
+        settle(e + 1, second, 1, row_s2, row_n2, *gained(push_second, e + 1), e + 2)
         scatter(second, 1, row_s2, row_n2)
         between(1)
 
@@ -269,9 +283,8 @@
             side_n[c, pl.ds(i, 1), :] = value[ny - 1 : ny]
 
         loop(0, nx, step_image)
-        arrive(e + 2)
-        correct(
-            image, 0, side_s.at[c], side_n.at[c],
+        settle(
+            e + 2, image, 0, side_s.at[c], side_n.at[c],
             lambda s: -(face_x[s] * halo_x[e + 2, s]),
             lambda s: -(face_y[s] * halo_y[e + 2, s]),
         )
@@ -357,8 +370,6 @@
         w = w_next[i]
         r = right_ref[i] - a0 * w0[i]
         u = u0[i + 1] - a0 * m0[i + 1]
-        r_next[i] = r
-        u_next[i] = u
         return sums[0] + fold(r * u), sums[1] + fold(w * u)
 
     def third_plane(i, sums):
@@ -377,18 +388,44 @@
     b = g1 / g0
     a1 = g1 / (h1 - b * g1 / a0)
 
-    def finish(i, _):
-        u = u_next[i]
-        x_out[i] = a0 * u0[i + 1] + a1 * (u + b * u0[i + 1])
-        r_out[i] = r_next[i] - a1 * (w_next[i] + b * w0[i])
-        u_out[i] = u - a1 * (seconds[2, i + 1] + b * m0[i + 1])
-        w_out[i] = w_next[i] - a1 * (images[2, i] + b * n0[i])
-
-    loop(0, nx, finish)
-
-    for e, sources in sent:
-        for side in range(4):
-            pl.when(has[side])(functools.partial(lambda c: c.wait_send(), copy_of(e, side, sources[side])))
+    for k, value in enumerate((a0, a1, b)):
+        steps[k] = jnp.broadcast_to(value, (8, 128))
+
+    for e, side, source in sent:
+        pl.when(has[side])(functools.partial(lambda c: c.wait_send(), copy_of(e, side, source)))
+
+
+def finish(parts, right_ref, seconds, images, steps, x_out, r_out, u_out, w_out, right, held, in_sem, out_sem):
+    nx = right.shape[0]
+    span = nx // parts
+    fetch = [
+        pltpu.make_async_copy(right_ref.at[pl.ds(p * span, span)], right.at[pl.ds(p * span, span)], in_sem.at[p])
+        for p in range(parts)
+    ]
+    for copy in fetch:
+        copy.start()
+    a0, a1, b = (steps[k][0:1, 0:1] for k in range(3))
+    stores = []
+    for p in range(parts):
+        fetch[p].wait()
+
+        def plane(i, _):
+            u0, w0, m0, n0 = seconds[0, i + 1], images[0, i], seconds[1, i + 1], images[1, i]
+            u1 = u0 - a0 * m0
+            w1 = w0 - a0 * n0
+            held[0, i] = a0 * u0 + a1 * (u1 + b * u0)
+            held[1, i] = (right[i] - a0 * w0) - a1 * (w1 + b * w0)
+            held[2, i] = u1 - a1 * (seconds[2, i + 1] + b * m0)
+            held[3, i] = w1 - a1 * (images[2, i] + b * n0)
+
+        loop(p * span, (p + 1) * span, plane)
+        for k, out in enumerate((x_out, r_out, u_out, w_out)):
+            rows = pl.ds(p * span, span)
+            copy = pltpu.make_async_copy(held.at[k, rows], out.at[rows], out_sem.at[k, p])
+            copy.start()
+            stores.append(copy)
+    for copy in stores:
+        copy.wait()
 
 
 def solution(mesh):
@@ -403,15 +440,14 @@
         packed_one = pltpu.VMEM((nx, nz), f32)
         sides = pltpu.VMEM((5, nx, nz), f32)
         whole = pl.BlockSpec(memory_space=pltpu.VMEM)
-        return pl.pallas_call(
+        seconds, images, steps = pl.pallas_call(
             functools.partial(kernel, ngx, ngy),
-            out_shape=[jax.ShapeDtypeStruct((nx, ny, nz), f32)] * 4,
+            out_shape=[three, pltpu.VMEM((3, nx, ny, nz), f32), pltpu.VMEM((3, 8, 128), f32)],
             in_specs=[whole, whole, pl.BlockSpec(memory_space=pltpu.SMEM)],
-            out_specs=[whole] * 4,
+            out_specs=[whole] * 3,
             scratch_shapes=[
                 block, pltpu.VMEM((nx + 1, ny, nz), f32), block, block, block, block,
-                three, three, three, pltpu.VMEM((3, nx, ny, nz), f32),
-                block, block, block,
+                three, three, block,
                 packed, packed, packed_one, packed_one, sides, sides,
                 pltpu.VMEM((2, ny, nz), f32), pltpu.VMEM((2, nx, nz), f32),
                 pltpu.VMEM((2, ny, nz), f32), pltpu.VMEM((2, nx, nz), f32),
@@ -422,9 +458,22 @@
                 pltpu.SemaphoreType.DMA((2, ngy)), pltpu.SemaphoreType.DMA((2, ngy)),
             ],
             compiler_params=pltpu.CompilerParams(
-                collective_id=0, has_side_effects=True, vmem_limit_bytes=56 * 1024 * 1024
+                collective_id=0, has_side_effects=True, vmem_limit_bytes=40 * 1024 * 1024
             ),
         )(right_side, phase, table)
+        parts = next(p for p in (8, 4, 2, 1) if nx % p == 0)
+        anywhere = pl.BlockSpec(memory_space=pl.ANY)
+        return pl.pallas_call(
+            functools.partial(finish, parts),
+            out_shape=[jax.ShapeDtypeStruct((nx, ny, nz), f32)] * 4,
+            in_specs=[anywhere, whole, whole, whole],
+            out_specs=[anywhere] * 4,
+            scratch_shapes=[
+                block, pltpu.VMEM((4, nx, ny, nz), f32),
+                pltpu.SemaphoreType.DMA((parts,)), pltpu.SemaphoreType.DMA((4, parts)),
+            ],
+            compiler_params=pltpu.CompilerParams(vmem_limit_bytes=20 * 1024 * 1024),
+        )(right_side, seconds, images, steps)
 
     spec = P("gx", "gy", None)
     return jax.shard_map(

time: 54 us -> 49.4 us (0.915)
  local copies, waits for them, and re-layouts: 6.57 us -> 3.1 us
  Pallas kernels: 45.9 us -> 44.6 us
    unnamed x10 -> x6, local copies, waits for them, and re-layouts: 6.57 us -> 3.1 us
    pallas_call x1 -> x2, Pallas kernels: 45.9 us -> 44.6 us  [the longest x1 40.8 us: local(): pl.pallas_call(functools.partial(kernel, ngx, ngy), out_shape=[three, plt...]
where the time goes in v2:
time: 49.4 us; the launch traced here: 48.4 us
  Pallas kernels  44.6 us (90%)
  local copies, waits for them, and re-layouts  3.1 us (6%)
  between operations  0.65 us (1%)
    pallas_call x1, Pallas kernels, local(): pl.pallas_call(functools.partial(kernel, ngx, ngy), out_shape=[three, plt...  40.8 us
    pallas_call x1, Pallas kernels, local(): pl.pallas_call(functools.partial(finish, parts), out_shape=[jax.ShapeDtyp...  3.83 us
    unnamed x6, local copies, waits for them, and re-layouts  3.1 us

profile of v2, /device:TPU:0, one launch (start us, length us, event | category | flops | bytes accessed | tf_op | source)
XLA Modules:
  0.0 48.4 jit_solution(18122129965751059193)
XLA Ops:
  0.6 0.0 copy-start
  0.6 1.2 %copy-done = f32[32,32,256]{2,1,0:T(8,128)S(1)} copy-done((f32[32,32,256]{2,1,0:T(8,128)S(1)}, f32[32,32,256]{2,1,0:T(8,128)}, u32[]{:S(2)}) %copy-start) | copy-done | bytes 1048600
  1.9 0.0 copy-start.1
  1.9 1.2 %copy-done.1 = s32[32,32,256]{2,1,0:T(8,128)S(1)} copy-done((s32[32,32,256]{2,1,0:T(8,128)S(1)}, s32[32,32,256]{2,1,0:T(8,128)}, u32[]{:S(2)}) %copy-start.1) | copy-done | bytes 1048600
  3.1 0.0 copy-start.2
  3.1 0.7 %copy-done.2 = f32[4]{0:T(128)S(1)} copy-done((f32[4]{0:T(128)S(1)}, f32[4]{0:T(128)}, u32[]{:S(2)}) %copy-start.2) | copy-done | bytes 40
  3.7 40.8 %shard_map.66 = (f32[3,34,32,256]{3,2,1,0:T(8,128)S(1)}, f32[3,32,32,256]{3,2,1,0:T(8,128)S(1)}, f32[3,8,128]{2,1,0:T(8,128)S(1)}) custom-call(f32[32,32,256]{2,1,0:T(8,128)S(1)} %copy-done, s32[32,32,256]{2,1,0:T(8,128)S(1)} %copy-done.1, f32[4]{0:T(128)S(1)} %copy-done.2), custom_call_target="tpu_custom_call" | custom-call | tf_op jit(solution)/shard_map/pallas_call | solution.py:443
  44.5 3.8 %shard_map.67 = (f32[32,32,256]{2,1,0:T(8,128)}, f32[32,32,256]{2,1,0:T(8,128)}, f32[32,32,256]{2,1,0:T(8,128)}, f32[32,32,256]{2,1,0:T(8,128)}) custom-call(f32[32,32,256]{2,1,0:T(8,128)S(1)} %copy-done, f32[3,34,32,256]{3,2,1,0:T(8,128)S(1)} %get-tuple-element.7.seconds, f32[3,32,32,256]{3,2,1,0:T(8,128)S(1)} %get-tuple-element.8.images, ...), custom_call_target="tpu_custom_call" | custom-call | tf_op jit(solution)/shard_map/pallas_call | solution.py:466
Async XLA Ops:
  0.6 1.2 %copy-start = (f32[32,32,256]{2,1,0:T(8,128)S(1)}, f32[32,32,256]{2,1,0:T(8,128)}, u32[]{:S(2)}) copy-start(f32[32,32,256]{2,1,0:T(8,128)} %right_ref.3) | copy-start | bytes 3145732
  1.9 1.2 %copy-start.1 = (s32[32,32,256]{2,1,0:T(8,128)S(1)}, s32[32,32,256]{2,1,0:T(8,128)}, u32[]{:S(2)}) copy-start(s32[32,32,256]{2,1,0:T(8,128)} %phase_ref.1) | copy-start | bytes 3145732
  3.1 0.7 %copy-start.2 = (f32[4]{0:T(128)S(1)}, f32[4]{0:T(128)}, u32[]{:S(2)}) copy-start(f32[4]{0:T(128)} %table_ref.1) | copy-start | bytes 52

commit v3 on v2

--- a/solution.py
+++ b/solution.py
@@ -58,19 +58,33 @@
 
 def kernel(
     ngx, ngy,
+    right_in, phase_in, table_in,
+    x_out, r_out, u_out, w_out,
     right_ref, phase_ref, table_ref,
-    seconds, images, steps,
+    seconds, images,
     rho, cx, cs, cd, diag, inv,
     ys, firsts, w_next,
     pack_s, pack_n, inv_s, inv_n, side_s, side_n,
     face_x, face_y, gain_x, gain_y,
     halo_x, halo_y, red_x, red_y,
-    send_sem, recv_sem, rx_send, rx_recv, ry_send, ry_recv,
+    send_sem, recv_sem, rx_send, rx_recv, ry_send, ry_recv, in_sem,
 ):
     nx, ny, nz = right_ref.shape
     gx = lax.axis_index("gx")
     gy = lax.axis_index("gy")
     has = (gx > 0, gx < ngx - 1, gy > 0, gy < ngy - 1)
+
+    parts = next(p for p in (4, 2, 1) if nx % p == 0)
+    span = nx // parts
+    fetch_table = pltpu.make_async_copy(table_in, table_ref, in_sem.at[parts + 1])
+    fetch_table.start()
+    fetches = []
+    for p in range(parts):
+        rows = pl.ds(p * span, span)
+        fetches.append(pltpu.make_async_copy(phase_in.at[rows], phase_ref.at[rows], in_sem.at[p]))
+        fetches[p].start()
+    fetch_right = pltpu.make_async_copy(right_in, right_ref, in_sem.at[parts])
+    fetch_right.start()
 
     barrier = pltpu.get_barrier_semaphore()
     for k in range(1, ngx):
@@ -111,6 +125,8 @@
             )
             pl.when(has[side])(functools.partial(lambda c: c.wait_recv(), dummy))
 
+    fetch_table.wait()
+
     t1, t2, t3 = (jnp.full((1, 1), table_ref[k], jnp.float32) for k in (1, 2, 3))
     q0 = 1.0 / jnp.full((1, 1), table_ref[0], jnp.float32)
     q1, q2, q3 = 1.0 / t1, 1.0 / t2, 1.0 / t3
@@ -130,11 +146,10 @@
         rho[i] = value
         pack_s[0, pl.ds(i, 1), :] = value[0:1]
         pack_n[0, pl.ds(i, 1), :] = value[ny - 1 : ny]
-        right = right_ref[i]
-        side_s[4, pl.ds(i, 1), :] = right[0:1]
-        side_n[4, pl.ds(i, 1), :] = right[ny - 1 : ny]
-
-    loop(0, nx, lookup_plane)
+
+    for p in range(parts):
+        fetches[p].wait()
+        loop(p * span, (p + 1) * span, lookup_plane)
     pl.semaphore_wait(barrier, ngx - 1 + ngy - 1)
     send(0, 2, pack_s.at[0])
     send(0, 3, pack_n.at[0])
@@ -155,6 +170,14 @@
         cx[i] = 2.0 / (rho[i - 1] + rho[i])
 
     loop(1, nx, couple_x)
+    fetch_right.wait()
+
+    def right_rows(i, _):
+        right = right_ref[i]
+        side_s[4, pl.ds(i, 1), :] = right[0:1]
+        side_n[4, pl.ds(i, 1), :] = right[ny - 1 : ny]
+
+    loop(0, nx, right_rows)
 
     def couple_rest(i, _):
         here = rho[i]
@@ -249,8 +272,8 @@
             lambda s: (scale * gain_y[s]) * halo_y[e, s],
         )
 
-    def composite(c, e, between):
-        y, first, second, image = ys.at[c], firsts.at[c], seconds.at[c], images.at[c]
+    def composite(c, e, between, image, image_of=lambda i, value: value, scale=lambda: -1.0):
+        y, first, second = ys.at[c], firsts.at[c], seconds.at[c]
 
         def step_first(i, _):
             value = own_first * y[i + 1] + near_first * (inv[i] * near(y, i))
@@ -277,7 +300,7 @@
         between(1)
 
         def step_image(i, _):
-            value = diag[i] * second[i + 1] - near(second, i)
+            value = image_of(i, diag[i] * second[i + 1] - near(second, i))
             image[i] = value
             side_s[c, pl.ds(i, 1), :] = value[0:1]
             side_n[c, pl.ds(i, 1), :] = value[ny - 1 : ny]
@@ -285,8 +308,8 @@
         loop(0, nx, step_image)
         settle(
             e + 2, image, 0, side_s.at[c], side_n.at[c],
-            lambda s: -(face_x[s] * halo_x[e + 2, s]),
-            lambda s: -(face_y[s] * halo_y[e + 2, s]),
+            lambda s: scale() * (face_x[s] * halo_x[e + 2, s]),
+            lambda s: scale() * (face_y[s] * halo_y[e + 2, s]),
         )
 
     def reduce_start(buffer, axis, position, count, send_sems, recv_sems):
@@ -338,7 +361,7 @@
         ys[0, i + 1] = right_ref[i] * value
 
     loop(1, nx - 1, start_plane)
-    composite(0, 1, lambda k: None)
+    composite(0, 1, lambda k: None, images.at[0])
 
     w0, u0 = images.at[0], seconds.at[0]
     send_y(4, ys.at[1], lambda p: w0[p], side_s[0], side_n[0])
@@ -356,7 +379,7 @@
         u = u0[plane + 1]
         sums = (sums[0] + fold(right_ref[plane] * u), sums[1] + fold(w0[plane] * u))
     put_sums(0, loop(1, nx - 1, second_plane, sums))
-    composite(1, 4, lambda k: relay(0) if k == 0 else None)
+    composite(1, 4, lambda k: relay(0) if k == 0 else None, images.at[1])
     g0, h0 = take_sums(0)
     a0 = g0 / h0
 
@@ -382,49 +405,48 @@
     for plane in (0, nx - 1):
         sums = advance(plane, sums)
     put_sums(1, loop(1, nx - 1, third_plane, sums))
-    composite(2, 7, lambda k: relay(1) if k == 0 else None)
-    scatter(images.at[2], 0, side_s.at[2], side_n.at[2])
-    g1, h1 = take_sums(1)
-    b = g1 / g0
-    a1 = g1 / (h1 - b * g1 / a0)
-
-    for k, value in enumerate((a0, a1, b)):
-        steps[k] = jnp.broadcast_to(value, (8, 128))
+    found = []
+
+    def last_between(k):
+        if k == 0:
+            relay(1)
+            return
+        g1, h1 = take_sums(1)
+        b = g1 / g0
+        a1 = g1 / (h1 - b * g1 / a0)
+        found.extend((a1, b))
+
+        def finish(i, _):
+            u, m = u0[i + 1], m0[i + 1]
+            u_next = u - a0 * m
+            x_out[i] = a0 * u + a1 * (u_next + b * u)
+            u_out[i] = u_next - a1 * (seconds[2, i + 1] + b * m)
+            w = w0[i]
+            r_out[i] = (right_ref[i] - a0 * w) - a1 * (w_next[i] + b * w)
+
+        loop(0, nx, finish)
+
+    composite(
+        2, 7, last_between, w_out,
+        lambda i, value: w_next[i] - found[0] * (value + found[1] * n0[i]),
+        lambda: found[0],
+    )
+    scatter(w_out, 0, side_s.at[2], side_n.at[2])
 
     for e, side, source in sent:
         pl.when(has[side])(functools.partial(lambda c: c.wait_send(), copy_of(e, side, source)))
 
 
-def finish(parts, right_ref, seconds, images, steps, x_out, r_out, u_out, w_out, right, held, in_sem, out_sem):
-    nx = right.shape[0]
-    span = nx // parts
-    fetch = [
-        pltpu.make_async_copy(right_ref.at[pl.ds(p * span, span)], right.at[pl.ds(p * span, span)], in_sem.at[p])
-        for p in range(parts)
-    ]
-    for copy in fetch:
-        copy.start()
-    a0, a1, b = (steps[k][0:1, 0:1] for k in range(3))
-    stores = []
-    for p in range(parts):
-        fetch[p].wait()
-
-        def plane(i, _):
-            u0, w0, m0, n0 = seconds[0, i + 1], images[0, i], seconds[1, i + 1], images[1, i]
-            u1 = u0 - a0 * m0
-            w1 = w0 - a0 * n0
-            held[0, i] = a0 * u0 + a1 * (u1 + b * u0)
-            held[1, i] = (right[i] - a0 * w0) - a1 * (w1 + b * w0)
-            held[2, i] = u1 - a1 * (seconds[2, i + 1] + b * m0)
-            held[3, i] = w1 - a1 * (images[2, i] + b * n0)
-
-        loop(p * span, (p + 1) * span, plane)
-        for k, out in enumerate((x_out, r_out, u_out, w_out)):
+def deliver(parts, *refs):
+    held, outs, sems = refs[:4], refs[4:8], refs[8]
+    span = held[0].shape[0] // parts
+    copies = []
+    for k in range(4):
+        for p in range(parts):
             rows = pl.ds(p * span, span)
-            copy = pltpu.make_async_copy(held.at[k, rows], out.at[rows], out_sem.at[k, p])
-            copy.start()
-            stores.append(copy)
-    for copy in stores:
+            copies.append(pltpu.make_async_copy(held[k].at[rows], outs[k].at[rows], sems.at[k, p]))
+            copies[-1].start()
+    for copy in copies:
         copy.wait()
 
 
@@ -440,12 +462,15 @@
         packed_one = pltpu.VMEM((nx, nz), f32)
         sides = pltpu.VMEM((5, nx, nz), f32)
         whole = pl.BlockSpec(memory_space=pltpu.VMEM)
-        seconds, images, steps = pl.pallas_call(
+        far = pl.BlockSpec(memory_space=pltpu.HBM)
+        held = pl.pallas_call(
             functools.partial(kernel, ngx, ngy),
-            out_shape=[three, pltpu.VMEM((3, nx, ny, nz), f32), pltpu.VMEM((3, 8, 128), f32)],
-            in_specs=[whole, whole, pl.BlockSpec(memory_space=pltpu.SMEM)],
-            out_specs=[whole] * 3,
+            out_shape=[block] * 4,
+            in_specs=[far] * 3,
+            out_specs=[whole] * 4,
             scratch_shapes=[
+                block, pltpu.VMEM((nx, ny, nz), jnp.int32), pltpu.SMEM(table.shape, f32),
+                three, pltpu.VMEM((2, nx, ny, nz), f32),
                 block, pltpu.VMEM((nx + 1, ny, nz), f32), block, block, block, block,
                 three, three, block,
                 packed, packed, packed_one, packed_one, sides, sides,
@@ -456,24 +481,21 @@
                 pltpu.SemaphoreType.DMA((EXCHANGES, 4)), pltpu.SemaphoreType.DMA((EXCHANGES, 4)),
                 pltpu.SemaphoreType.DMA((2, ngx)), pltpu.SemaphoreType.DMA((2, ngx)),
                 pltpu.SemaphoreType.DMA((2, ngy)), pltpu.SemaphoreType.DMA((2, ngy)),
+                pltpu.SemaphoreType.DMA((6,)),
             ],
             compiler_params=pltpu.CompilerParams(
-                collective_id=0, has_side_effects=True, vmem_limit_bytes=40 * 1024 * 1024
+                collective_id=0, has_side_effects=True, vmem_limit_bytes=59 * 1024 * 1024 + 512 * 1024
             ),
         )(right_side, phase, table)
-        parts = next(p for p in (8, 4, 2, 1) if nx % p == 0)
-        anywhere = pl.BlockSpec(memory_space=pl.ANY)
+        parts = next(p for p in (2, 1) if nx % p == 0)
         return pl.pallas_call(
-            functools.partial(finish, parts),
+            functools.partial(deliver, parts),
             out_shape=[jax.ShapeDtypeStruct((nx, ny, nz), f32)] * 4,
-            in_specs=[anywhere, whole, whole, whole],
-            out_specs=[anywhere] * 4,
-            scratch_shapes=[
-                block, pltpu.VMEM((4, nx, ny, nz), f32),
-                pltpu.SemaphoreType.DMA((parts,)), pltpu.SemaphoreType.DMA((4, parts)),
-            ],
-            compiler_params=pltpu.CompilerParams(vmem_limit_bytes=20 * 1024 * 1024),
-        )(right_side, seconds, images, steps)
+            in_specs=[whole] * 4,
+            out_specs=[far] * 4,
+            scratch_shapes=[pltpu.SemaphoreType.DMA((4, parts))],
+            compiler_params=pltpu.CompilerParams(vmem_limit_bytes=16 * 1024 * 1024),
+        )(*held)
 
     spec = P("gx", "gy", None)
     return jax.shard_map(

time: 49.4 us -> 44.4 us (0.90); the launches traced: 48.4 us -> 44.3 us
  local copies, waits for them, and re-layouts: 3.1 us -> 0 us
  Pallas kernels: 44.6 us -> 43.6 us
    unnamed x6 -> x0, local copies, waits for them, and re-layouts: 3.1 us -> none
    pallas_call x2, Pallas kernels: 44.6 us -> 43.6 us  [the longest x1 41.6 us: local(): pl.pallas_call(functools.partial(kernel, ngx, ngy), out_shape=[block] * 4...]
where the time goes in v3:
time: 44.4 us; the launch traced here: 44.3 us
  Pallas kernels  43.6 us (98%)
  between operations  0.64 us (1%)
    pallas_call x1, Pallas kernels, local(): pl.pallas_call(functools.partial(kernel, ngx, ngy), out_shape=[block] * 4...  41.6 us
    pallas_call x1, Pallas kernels, local(): pl.pallas_call(functools.partial(deliver, parts), out_shape=[jax.ShapeDty...  2.07 us

profile of v3, /device:TPU:0, one launch (start us, length us, event | category | flops | bytes accessed | tf_op | source)
XLA Modules:
  0.0 44.3 jit_solution(6807846995707245434)
XLA Ops:
  0.6 41.6 %shard_map.66 = (f32[32,32,256]{2,1,0:T(8,128)S(1)}, f32[32,32,256]{2,1,0:T(8,128)S(1)}, f32[32,32,256]{2,1,0:T(8,128)S(1)}, f32[32,32,256]{2,1,0:T(8,128)S(1)}) custom-call(f32[32,32,256]{2,1,0:T(8,128)} %right_in.1, s32[32,32,256]{2,1,0:T(8,128)} %phase_in.1, f32[4]{0:T(128)} %table_in.1), custom_call_target="tpu_custom_call" | custom-call | tf_op jit(solution)/shard_map/pallas_call | solution.py:466
  42.2 2.1 %shard_map.67 = (f32[32,32,256]{2,1,0:T(8,128)}, f32[32,32,256]{2,1,0:T(8,128)}, f32[32,32,256]{2,1,0:T(8,128)}, f32[32,32,256]{2,1,0:T(8,128)}) custom-call(f32[32,32,256]{2,1,0:T(8,128)S(1)} %get-tuple-element.8.refs_0_, f32[32,32,256]{2,1,0:T(8,128)S(1)} %get-tuple-element.9.refs_1_, f32[32,32,256]{2,1,0:T(8,128)S(1)} %get-tuple-element.10.refs_2_, ...), custom_call_target="tpu_custom_call" | custom-call | tf_op jit(solution)/shard_map/pallas_call | solution.py:491

commit v4 on v3

--- a/solution.py
+++ b/solution.py
@@ -26,7 +26,8 @@
 own_second = 1.0 + keep_second - push_second
 base_second = push_second - keep_second * start_scale
 
-EXCHANGES = 10
+EXCHANGES = 11
+SCALES = 10
 
 
 def loop(low, high, body, carry=None):
@@ -61,10 +62,10 @@
     right_in, phase_in, table_in,
     x_out, r_out, u_out, w_out,
     right_ref, phase_ref, table_ref,
-    seconds, images,
-    rho, cx, cs, cd, diag, inv,
-    ys, firsts, w_next,
-    pack_s, pack_n, inv_s, inv_n, side_s, side_n,
+    seconds, n0,
+    rho, cx, cs, cd, root, scale,
+    ys, firsts,
+    pack_s, pack_n, side_s, side_n,
     face_x, face_y, gain_x, gain_y,
     halo_x, halo_y, red_x, red_y,
     send_sem, recv_sem, rx_send, rx_recv, ry_send, ry_recv, in_sem,
@@ -191,7 +192,7 @@
         cd[i] = inner
         up = jnp.where(lane == nz - 1, last, pltpu.roll(inner, nz - 1, 1))
         d = cx[i] + cx[i + 1] + south + pltpu.roll(south, ny - 1, 0) + down + up
-        diag[i] = d
+        root[i] = d
         side_s[3, pl.ds(i, 1), :] = d[0:1]
         side_n[3, pl.ds(i, 1), :] = d[ny - 1 : ny]
 
@@ -230,87 +231,126 @@
     face_y[1] = 2.0 / (pack_n[0] + halo_y[0, 1])
     ds_, dn_ = side_s.at[3], side_n.at[3]
     for side, plane in ((0, 0), (1, nx - 1)):
-        whole = diag[plane] + face_x[side]
-        diag[plane] = whole
+        whole = root[plane] + face_x[side]
+        root[plane] = whole
         ds_[plane : plane + 1, :] = whole[0:1]
         dn_[plane : plane + 1, :] = whole[ny - 1 : ny]
     ds_[...] = ds_[...] + face_y[0]
     dn_[...] = dn_[...] + face_y[1]
     for plane in (0, nx - 1):
-        diag[plane, 0:1, :] = ds_[plane : plane + 1, :]
-        diag[plane, ny - 1 : ny, :] = dn_[plane : plane + 1, :]
-    inv_s[...] = 1.0 / ds_[...]
-    inv_n[...] = 1.0 / dn_[...]
+        root[plane, 0:1, :] = ds_[plane : plane + 1, :]
+        root[plane, ny - 1 : ny, :] = dn_[plane : plane + 1, :]
+
+    def inverse_root(d):
+        guess = lax.rsqrt(d)
+        return guess * (1.5 - 0.5 * (d * guess) * guess)
+
+    for k, (packed, rows) in enumerate(((pack_s, ds_), (pack_n, dn_))):
+        packed[SCALES] = inverse_root(rows[...])
+        send(SCALES, 2 + k, packed.at[SCALES])
     for side, plane in ((0, 0), (1, nx - 1)):
-        inv[plane] = 1.0 / diag[plane]
-        gain_x[side] = face_x[side] * inv[plane]
-    gain_y[0] = face_y[0] * inv_s[...]
-    gain_y[1] = face_y[1] * inv_n[...]
-
-    def near(f, i):
-        here = f[i + 1]
-        south = cs[i]
-        down = cd[i]
+        scale[plane] = inverse_root(root[plane])
+        send(SCALES, side, scale.at[plane])
+    for k, (packed, rows) in enumerate(((pack_s, side_s), (pack_n, side_n))):
+        packed[1] = rows[4] * packed[SCALES]
+        send(1, 2 + k, packed.at[1])
+    for side, plane in ((0, 0), (1, nx - 1)):
+        ys[0, plane + 1] = right_ref[plane] * scale[plane]
+        send(1, side, ys.at[0, plane + 1])
+    scatter(root, 0, ds_, dn_)
+
+    def scale_plane(i, _):
+        d = root[i]
+        value = inverse_root(d)
+        scale[i] = value
+        root[i] = d * value
+        ys[0, i + 1] = right_ref[i] * value
+
+    loop(1, nx - 1, scale_plane)
+    for plane in (0, nx - 1):
+        root[plane] = root[plane] * scale[plane]
+    for rows, packed in ((ds_, pack_s), (dn_, pack_n)):
+        rows[...] = rows[...] * packed[SCALES]
+
+    def scale_couplings(i, _):
+        here = scale[i]
+        cx[i] = cx[i] * (here * scale[i - 1])
+        cs[i] = cs[i] * (here * pltpu.roll(here, 1, 0))
+        cd[i] = cd[i] * (here * pltpu.roll(here, 1, 1))
+
+    here = scale[0]
+    cs[0] = cs[0] * (here * pltpu.roll(here, 1, 0))
+    cd[0] = cd[0] * (here * pltpu.roll(here, 1, 1))
+    loop(1, nx, scale_couplings)
+
+    def sweep(f, leave):
+        unroll = next(u for u in (4, 2, 1) if nx % u == 0)
+
+        def step(k, _):
+            base = k * unroll
+            west, here, to_west = f[base], f[base + 1], cx[base]
+            for j in range(unroll):
+                i = base + j
+                east, to_east, south, down = f[i + 2], cx[i + 1], cs[i], cd[i]
+                near = (
+                    (to_west * west + to_east * east)
+                    + (south * pltpu.roll(here, 1, 0) + pltpu.roll(south * here, ny - 1, 0))
+                    + (down * pltpu.roll(here, 1, 1) + pltpu.roll(down * here, nz - 1, 1))
+                )
+                leave(i, here, near)
+                west, here, to_west = here, east, to_east
+
+        lax.fori_loop(0, nx // unroll, step, None)
+
+    def gained(factor, e):
         return (
-            (cx[i] * f[i] + cx[i + 1] * f[i + 2])
-            + (south * pltpu.roll(here, 1, 0) + pltpu.roll(south * here, ny - 1, 0))
-            + (down * pltpu.roll(here, 1, 1) + pltpu.roll(down * here, nz - 1, 1))
+            lambda s: (factor * gain_x[s]) * halo_x[e, s],
+            lambda s: (factor * gain_y[s]) * halo_y[e, s],
         )
 
-    def send_y(e, y, plane_value, value_s, value_n):
-        pack_s[e] = value_s * inv_s[...]
-        send(e, 2, pack_s.at[e])
-        pack_n[e] = value_n * inv_n[...]
-        send(e, 3, pack_n.at[e])
-        for side, plane in ((0, 0), (1, nx - 1)):
-            y[plane + 1] = plane_value(plane) * inv[plane]
-            send(e, side, y.at[plane + 1])
-
-    def gained(scale, e):
-        return (
-            lambda s: (scale * gain_x[s]) * halo_x[e, s],
-            lambda s: (scale * gain_y[s]) * halo_y[e, s],
-        )
-
-    def composite(c, e, between, image, image_of=lambda i, value: value, scale=lambda: -1.0):
-        y, first, second = ys.at[c], firsts.at[c], seconds.at[c]
-
-        def step_first(i, _):
-            value = own_first * y[i + 1] + near_first * (inv[i] * near(y, i))
+    def put_rows(rows_s, rows_n, i, value):
+        rows_s[pl.ds(i, 1), :] = value[0:1]
+        rows_n[pl.ds(i, 1), :] = value[ny - 1 : ny]
+
+    def composite(c, e, between, image, image_first, rows, adds, image_of=lambda i, value: value, e_out=None):
+        v, first, second = ys.at[c], firsts.at[c], seconds.at[c]
+        rows_1 = pack_s.at[e + 1], pack_n.at[e + 1]
+        rows_2 = pack_s.at[e + 2], pack_n.at[e + 2]
+
+        def leave_first(i, here, near):
+            value = own_first * here + near_first * near
             first[i + 1] = value
-            pack_s[e + 1, pl.ds(i, 1), :] = value[0:1]
-            pack_n[e + 1, pl.ds(i, 1), :] = value[ny - 1 : ny]
-
-        loop(0, nx, step_first)
-        row_s, row_n = pack_s.at[e + 1], pack_n.at[e + 1]
-        settle(e, first, 1, row_s, row_n, *gained(near_first, e), e + 1)
-        scatter(first, 1, row_s, row_n)
+            put_rows(*rows_1, i, value)
+
+        sweep(v, leave_first)
+        if c == 0:
+            arrive(SCALES, range(4))
+            for side, plane in ((0, 0), (1, nx - 1)):
+                gain_x[side] = (face_x[side] * scale[plane]) * halo_x[SCALES, side]
+            gain_y[0] = (face_y[0] * pack_s[SCALES]) * halo_y[SCALES, 0]
+            gain_y[1] = (face_y[1] * pack_n[SCALES]) * halo_y[SCALES, 1]
+        settle(e, first, 1, *rows_1, *gained(near_first, e), e + 1)
+        scatter(first, 1, *rows_1)
         between(0)
 
-        def step_second(i, _):
-            value = own_second * first[i + 1] + base_second * y[i + 1] + push_second * (inv[i] * near(first, i))
+        def leave_second(i, here, near):
+            value = own_second * here + (base_second * v[i + 1] + push_second * near)
             second[i + 1] = value
-            pack_s[e + 2, pl.ds(i, 1), :] = value[0:1]
-            pack_n[e + 2, pl.ds(i, 1), :] = value[ny - 1 : ny]
-
-        loop(0, nx, step_second)
-        row_s2, row_n2 = pack_s.at[e + 2], pack_n.at[e + 2]
-        settle(e + 1, second, 1, row_s2, row_n2, *gained(push_second, e + 1), e + 2)
-        scatter(second, 1, row_s2, row_n2)
+            put_rows(*rows_2, i, value)
+
+        sweep(first, leave_second)
+        settle(e + 1, second, 1, *rows_2, *gained(push_second, e + 1), e + 2)
+        scatter(second, 1, *rows_2)
         between(1)
 
-        def step_image(i, _):
-            value = image_of(i, diag[i] * second[i + 1] - near(second, i))
-            image[i] = value
-            side_s[c, pl.ds(i, 1), :] = value[0:1]
-            side_n[c, pl.ds(i, 1), :] = value[ny - 1 : ny]
-
-        loop(0, nx, step_image)
-        settle(
-            e + 2, image, 0, side_s.at[c], side_n.at[c],
-            lambda s: scale() * (face_x[s] * halo_x[e + 2, s]),
-            lambda s: scale() * (face_y[s] * halo_y[e + 2, s]),
-        )
+        def leave_image(i, here, near):
+            value = image_of(i, here - near)
+            image[image_first + i] = value
+            put_rows(*rows, i, value)
+
+        sweep(second, leave_image)
+        settle(e + 2, image, image_first, *rows, *adds(e + 2), e_out)
+        scatter(image, image_first, *rows)
 
     def reduce_start(buffer, axis, position, count, send_sems, recv_sems):
         for k in range(1, count):
@@ -352,59 +392,47 @@
         both = reduce_end(*over_y(t))
         return total(both[0:8]), total(both[8:16])
 
-    send_y(1, ys.at[0], lambda p: right_ref[p], side_s[4], side_n[4])
-    scatter(diag, 0, ds_, dn_)
-
-    def start_plane(i, _):
-        value = 1.0 / diag[i]
-        inv[i] = value
-        ys[0, i + 1] = right_ref[i] * value
-
-    loop(1, nx - 1, start_plane)
-    composite(0, 1, lambda k: None, images.at[0])
-
-    w0, u0 = images.at[0], seconds.at[0]
-    send_y(4, ys.at[1], lambda p: w0[p], side_s[0], side_n[0])
-    scatter(w0, 0, side_s.at[0], side_n.at[0])
+    def less(e):
+        return gained(-1.0, e)
+
+    composite(0, 1, lambda k: None, ys.at[1], 1, (pack_s.at[4], pack_n.at[4]), less, e_out=4)
+
+    r0, w0, w1 = ys.at[0], ys.at[1], ys.at[2]
+    u0, m0 = seconds.at[0], seconds.at[1]
     tile = jnp.zeros((8, 128), jnp.float32)
 
-    def second_plane(i, sums):
-        w = w0[i]
+    def first_sums(i, sums):
         u = u0[i + 1]
-        ys[1, i + 1] = w * inv[i]
-        return sums[0] + fold(right_ref[i] * u), sums[1] + fold(w * u)
+        return sums[0] + fold(r0[i + 1] * u), sums[1] + fold(w0[i + 1] * u)
+
+    put_sums(0, loop(0, nx, first_sums, (tile, tile)))
+    composite(
+        1, 4, lambda k: relay(0) if k == 0 else None, n0, 0, (side_s.at[1], side_n.at[1]), less
+    )
+    g0, h0 = take_sums(0)
+    a0 = g0 / h0
+
+    for k, (packed, rows) in enumerate(((pack_s, side_s), (pack_n, side_n))):
+        packed[7] = packed[4] - a0 * rows[1]
+        send(7, 2 + k, packed.at[7])
+    for side, plane in ((0, 0), (1, nx - 1)):
+        w1[plane + 1] = w0[plane + 1] - a0 * n0[plane]
+        send(7, side, w1.at[plane + 1])
+
+    def advance(i, sums, w):
+        r = r0[i + 1] - a0 * w0[i + 1]
+        u = u0[i + 1] - a0 * m0[i + 1]
+        return sums[0] + fold(r * u), sums[1] + fold(w * u)
+
+    def second_sums(i, sums):
+        w = w0[i + 1] - a0 * n0[i]
+        w1[i + 1] = w
+        return advance(i, sums, w)
 
     sums = (tile, tile)
     for plane in (0, nx - 1):
-        u = u0[plane + 1]
-        sums = (sums[0] + fold(right_ref[plane] * u), sums[1] + fold(w0[plane] * u))
-    put_sums(0, loop(1, nx - 1, second_plane, sums))
-    composite(1, 4, lambda k: relay(0) if k == 0 else None, images.at[1])
-    g0, h0 = take_sums(0)
-    a0 = g0 / h0
-
-    m0, n0 = seconds.at[1], images.at[1]
-    for plane in (0, nx - 1):
-        w_next[plane] = w0[plane] - a0 * n0[plane]
-    send_y(7, ys.at[2], lambda p: w_next[p], side_s[0] - a0 * side_s[1], side_n[0] - a0 * side_n[1])
-    scatter(n0, 0, side_s.at[1], side_n.at[1])
-
-    def advance(i, sums):
-        w = w_next[i]
-        r = right_ref[i] - a0 * w0[i]
-        u = u0[i + 1] - a0 * m0[i + 1]
-        return sums[0] + fold(r * u), sums[1] + fold(w * u)
-
-    def third_plane(i, sums):
-        w = w0[i] - a0 * n0[i]
-        w_next[i] = w
-        ys[2, i + 1] = w * inv[i]
-        return advance(i, sums)
-
-    sums = (tile, tile)
-    for plane in (0, nx - 1):
-        sums = advance(plane, sums)
-    put_sums(1, loop(1, nx - 1, third_plane, sums))
+        sums = advance(plane, sums, w1[plane + 1])
+    put_sums(1, loop(1, nx - 1, second_sums, sums))
     found = []
 
     def last_between(k):
@@ -417,21 +445,24 @@
         found.extend((a1, b))
 
         def finish(i, _):
-            u, m = u0[i + 1], m0[i + 1]
-            u_next = u - a0 * m
-            x_out[i] = a0 * u + a1 * (u_next + b * u)
-            u_out[i] = u_next - a1 * (seconds[2, i + 1] + b * m)
-            w = w0[i]
-            r_out[i] = (right_ref[i] - a0 * w) - a1 * (w_next[i] + b * w)
+            u, m, w, part = u0[i + 1], m0[i + 1], w0[i + 1], scale[i]
+            u1 = u - a0 * m
+            x_out[i] = part * (a0 * u + a1 * (u1 + b * u))
+            u_out[i] = part * (u1 - a1 * (seconds[2, i + 1] + b * m))
+            r_out[i] = right_ref[i] - root[i] * (a0 * w + a1 * (w1[i + 1] + b * w))
 
         loop(0, nx, finish)
 
+    def last_adds(e):
+        return (
+            lambda s: (found[0] * root[(0, nx - 1)[s]]) * (gain_x[s] * halo_x[e, s]),
+            lambda s: (found[0] * (ds_, dn_)[s][...]) * (gain_y[s] * halo_y[e, s]),
+        )
+
     composite(
-        2, 7, last_between, w_out,
-        lambda i, value: w_next[i] - found[0] * (value + found[1] * n0[i]),
-        lambda: found[0],
+        2, 7, last_between, w_out, 0, (side_s.at[2], side_n.at[2]), last_adds,
+        lambda i, value: root[i] * (w1[i + 1] - found[0] * (value + found[1] * n0[i])),
     )
-    scatter(w_out, 0, side_s.at[2], side_n.at[2])
 
     for e, side, source in sent:
         pl.when(has[side])(functools.partial(lambda c: c.wait_send(), copy_of(e, side, source)))
@@ -459,7 +490,6 @@
         block = pltpu.VMEM((nx, ny, nz), f32)
         three = pltpu.VMEM((3, nx + 2, ny, nz), f32)
         packed = pltpu.VMEM((EXCHANGES, nx, nz), f32)
-        packed_one = pltpu.VMEM((nx, nz), f32)
         sides = pltpu.VMEM((5, nx, nz), f32)
         whole = pl.BlockSpec(memory_space=pltpu.VMEM)
         far = pl.BlockSpec(memory_space=pltpu.HBM)
@@ -470,10 +500,10 @@
             out_specs=[whole] * 4,
             scratch_shapes=[
                 block, pltpu.VMEM((nx, ny, nz), jnp.int32), pltpu.SMEM(table.shape, f32),
-                three, pltpu.VMEM((2, nx, ny, nz), f32),
+                three, block,
                 block, pltpu.VMEM((nx + 1, ny, nz), f32), block, block, block, block,
-                three, three, block,
-                packed, packed, packed_one, packed_one, sides, sides,
+                three, three,
+                packed, packed, sides, sides,
                 pltpu.VMEM((2, ny, nz), f32), pltpu.VMEM((2, nx, nz), f32),
                 pltpu.VMEM((2, ny, nz), f32), pltpu.VMEM((2, nx, nz), f32),
                 pltpu.VMEM((EXCHANGES, 2, ny, nz), f32), pltpu.VMEM((EXCHANGES, 2, nx, nz), f32),

time: 44.4 us -> 45.3 us (1.020)
  Pallas kernels: 43.6 us -> 44.6 us
    pallas_call x1, Pallas kernels: 41.6 us -> 42.5 us  [local(): pl.pallas_call(functools.partial(kernel, ngx, ngy), out_shape=[block] * 4...]
where the time goes in v4:
time: 45.3 us; the launch traced here: 45.2 us
  Pallas kernels  44.6 us (98%)
  between operations  0.64 us (1%)
    pallas_call x1, Pallas kernels, local(): pl.pallas_call(functools.partial(kernel, ngx, ngy), out_shape=[block] * 4...  42.5 us
    pallas_call x1, Pallas kernels, local(): pl.pallas_call(functools.partial(deliver, parts), out_shape=[jax.ShapeDty...  2.07 us

profile of v4, /device:TPU:0, one launch (start us, length us, event | category | flops | bytes accessed | tf_op | source)
XLA Modules:
  0.0 45.2 jit_solution(7853995958240771549)
XLA Ops:
  0.6 42.5 %shard_map.66 = (f32[32,32,256]{2,1,0:T(8,128)S(1)}, f32[32,32,256]{2,1,0:T(8,128)S(1)}, f32[32,32,256]{2,1,0:T(8,128)S(1)}, f32[32,32,256]{2,1,0:T(8,128)S(1)}) custom-call(f32[32,32,256]{2,1,0:T(8,128)} %right_in.1, s32[32,32,256]{2,1,0:T(8,128)} %phase_in.1, f32[4]{0:T(128)} %table_in.1), custom_call_target="tpu_custom_call" | custom-call | tf_op jit(solution)/shard_map/pallas_call | solution.py:496
  43.1 2.1 %shard_map.67 = (f32[32,32,256]{2,1,0:T(8,128)}, f32[32,32,256]{2,1,0:T(8,128)}, f32[32,32,256]{2,1,0:T(8,128)}, f32[32,32,256]{2,1,0:T(8,128)}) custom-call(f32[32,32,256]{2,1,0:T(8,128)S(1)} %get-tuple-element.8.refs_0_, f32[32,32,256]{2,1,0:T(8,128)S(1)} %get-tuple-element.9.refs_1_, f32[32,32,256]{2,1,0:T(8,128)S(1)} %get-tuple-element.10.refs_2_, ...), custom_call_target="tpu_custom_call" | custom-call | tf_op jit(solution)/shard_map/pallas_call | solution.py:521

commit v5 on v3

--- a/solution.py
+++ b/solution.py
@@ -92,38 +92,52 @@
     for k in range(1, ngy):
         pl.semaphore_signal(barrier, inc=1, device_id={"gy": lax.rem(gy + k, ngy)}, device_id_type=MESH)
 
+    halves = 2 if nx % 16 == 0 else 1
+    half = nx // halves
+    pieces = {side: (None,) if side < 2 else tuple(range(halves)) for side in range(4)}
+
+    def piece_of(ref, piece):
+        return ref if piece is None else ref.at[pl.ds(piece * half, half)]
+
+    def slot(side, piece):
+        return side if piece is None else 2 + 2 * (side - 2) + piece
+
     def halo(e, side):
         return halo_x.at[e, side] if side < 2 else halo_y.at[e, side - 2]
 
-    def copy_of(e, side, src):
+    def copy_of(e, side, piece, src):
         axis, position = ("gx", gx) if side < 2 else ("gy", gy)
         step = -1 if side % 2 == 0 else 1
         return pltpu.make_async_remote_copy(
-            src_ref=src,
-            dst_ref=halo(e, side ^ 1),
-            send_sem=send_sem.at[e, side],
-            recv_sem=recv_sem.at[e, side ^ 1],
+            src_ref=piece_of(src, piece),
+            dst_ref=piece_of(halo(e, side ^ 1), piece),
+            send_sem=send_sem.at[e, slot(side, piece)],
+            recv_sem=recv_sem.at[e, slot(side ^ 1, piece)],
             device_id={axis: position + step},
             device_id_type=MESH,
         )
 
     sent = []
 
-    def send(e, side, source):
-        pl.when(has[side])(functools.partial(lambda c: c.start(), copy_of(e, side, source)))
-        sent.append((e, side, source))
-
-    def arrive(e, sides):
+    def send(e, side, source, chosen=None):
+        for piece in pieces[side] if chosen is None else (chosen,):
+            copy = copy_of(e, side, piece, source)
+            pl.when(has[side])(functools.partial(lambda c: c.start(), copy))
+            sent.append((side, copy))
+
+    def arrive(e, sides, chosen=None):
         for side in sides:
-            dummy = pltpu.make_async_remote_copy(
-                src_ref=halo(e, side),
-                dst_ref=halo(e, side),
-                send_sem=send_sem.at[e, side],
-                recv_sem=recv_sem.at[e, side],
-                device_id={"gx": gx, "gy": gy},
-                device_id_type=MESH,
-            )
-            pl.when(has[side])(functools.partial(lambda c: c.wait_recv(), dummy))
+            for piece in pieces[side] if chosen is None else (chosen,):
+                here = piece_of(halo(e, side), piece)
+                dummy = pltpu.make_async_remote_copy(
+                    src_ref=here,
+                    dst_ref=here,
+                    send_sem=send_sem.at[e, slot(side, piece)],
+                    recv_sem=recv_sem.at[e, slot(side, piece)],
+                    device_id={"gx": gx, "gy": gy},
+                    device_id_type=MESH,
+                )
+                pl.when(has[side])(functools.partial(lambda c: c.wait_recv(), dummy))
 
     fetch_table.wait()
 
@@ -213,10 +227,12 @@
             row_s[i : i + 1, :] = plane[0:1]
             row_n[i : i + 1, :] = plane[ny - 1 : ny]
         for k, rows in ((0, row_s), (1, row_n)):
-            arrive(e, (2 + k,))
-            rows[...] = rows[...] + add_y(k)
-            if e_out is not None:
-                send(e_out, 2 + k, rows)
+            for piece in pieces[2 + k]:
+                arrive(e, (2 + k,), piece)
+                part = slice(piece * half, (piece + 1) * half)
+                rows[part] = rows[part] + add_y(k, part)
+                if e_out is not None:
+                    send(e_out, 2 + k, rows, piece)
         for side, i in ((0, 0), (1, nx - 1)):
             ref[edge[side], 0:1, :] = row_s[i : i + 1, :]
             ref[edge[side], ny - 1 : ny, :] = row_n[i : i + 1, :]
@@ -269,7 +285,7 @@
     def gained(scale, e):
         return (
             lambda s: (scale * gain_x[s]) * halo_x[e, s],
-            lambda s: (scale * gain_y[s]) * halo_y[e, s],
+            lambda s, part: (scale * gain_y[s, part]) * halo_y[e, s, part],
         )
 
     def composite(c, e, between, image, image_of=lambda i, value: value, scale=lambda: -1.0):
@@ -309,7 +325,7 @@
         settle(
             e + 2, image, 0, side_s.at[c], side_n.at[c],
             lambda s: scale() * (face_x[s] * halo_x[e + 2, s]),
-            lambda s: scale() * (face_y[s] * halo_y[e + 2, s]),
+            lambda s, part: scale() * (face_y[s, part] * halo_y[e + 2, s, part]),
         )
 
     def reduce_start(buffer, axis, position, count, send_sems, recv_sems):
@@ -433,8 +449,8 @@
     )
     scatter(w_out, 0, side_s.at[2], side_n.at[2])
 
-    for e, side, source in sent:
-        pl.when(has[side])(functools.partial(lambda c: c.wait_send(), copy_of(e, side, source)))
+    for side, copy in sent:
+        pl.when(has[side])(functools.partial(lambda c: c.wait_send(), copy))
 
 
 def deliver(parts, *refs):
@@ -478,7 +494,7 @@
                 pltpu.VMEM((2, ny, nz), f32), pltpu.VMEM((2, nx, nz), f32),
                 pltpu.VMEM((EXCHANGES, 2, ny, nz), f32), pltpu.VMEM((EXCHANGES, 2, nx, nz), f32),
                 pltpu.VMEM((2, ngx, 16, 128), f32), pltpu.VMEM((2, ngy, 16, 128), f32),
-                pltpu.SemaphoreType.DMA((EXCHANGES, 4)), pltpu.SemaphoreType.DMA((EXCHANGES, 4)),
+                pltpu.SemaphoreType.DMA((EXCHANGES, 6)), pltpu.SemaphoreType.DMA((EXCHANGES, 6)),
                 pltpu.SemaphoreType.DMA((2, ngx)), pltpu.SemaphoreType.DMA((2, ngx)),
                 pltpu.SemaphoreType.DMA((2, ngy)), pltpu.SemaphoreType.DMA((2, ngy)),
                 pltpu.SemaphoreType.DMA((6,)),

time: 44.4 us -> 44.2 us (level)
  no operation moved by 1% of the time
where the time goes in v5:
time: 44.2 us; the launch traced here: 44 us
  Pallas kernels  43.4 us (98%)
  between operations  0.64 us (1%)
    pallas_call x1, Pallas kernels, local(): pl.pallas_call(functools.partial(kernel, ngx, ngy), out_shape=[block] * 4...  41.3 us
    pallas_call x1, Pallas kernels, local(): pl.pallas_call(functools.partial(deliver, parts), out_shape=[jax.ShapeDty...  2.07 us

profile of v5, /device:TPU:0, one launch (start us, length us, event | category | flops | bytes accessed | tf_op | source)
XLA Modules:
  0.0 44.0 jit_solution(14921353492980163307)
XLA Ops:
  0.6 41.3 %shard_map.66 = (f32[32,32,256]{2,1,0:T(8,128)S(1)}, f32[32,32,256]{2,1,0:T(8,128)S(1)}, f32[32,32,256]{2,1,0:T(8,128)S(1)}, f32[32,32,256]{2,1,0:T(8,128)S(1)}) custom-call(f32[32,32,256]{2,1,0:T(8,128)} %right_in.1, s32[32,32,256]{2,1,0:T(8,128)} %phase_in.1, f32[4]{0:T(128)} %table_in.1), custom_call_target="tpu_custom_call" | custom-call | tf_op jit(solution)/shard_map/pallas_call | solution.py:482
  42.0 2.1 %shard_map.67 = (f32[32,32,256]{2,1,0:T(8,128)}, f32[32,32,256]{2,1,0:T(8,128)}, f32[32,32,256]{2,1,0:T(8,128)}, f32[32,32,256]{2,1,0:T(8,128)}) custom-call(f32[32,32,256]{2,1,0:T(8,128)S(1)} %get-tuple-element.8.refs_0_, f32[32,32,256]{2,1,0:T(8,128)S(1)} %get-tuple-element.9.refs_1_, f32[32,32,256]{2,1,0:T(8,128)S(1)} %get-tuple-element.10.refs_2_, ...), custom_call_target="tpu_custom_call" | custom-call | tf_op jit(solution)/shard_map/pallas_call | solution.py:507

commit v6 on v5

--- a/solution.py
+++ b/solution.py
@@ -52,8 +52,8 @@
     return out
 
 
-def total(tile):
-    return jnp.sum(jnp.sum(tile, axis=0, keepdims=True), axis=1, keepdims=True)
+def total(row):
+    return jnp.sum(row, axis=1, keepdims=True)
 
 
 def kernel(
@@ -356,8 +356,8 @@
         return red_y.at[t], "gy", gy, ngy, ry_send.at[t], ry_recv.at[t]
 
     def put_sums(t, sums):
-        red_x[t, 0, 0:8, :] = sums[0]
-        red_x[t, 0, 8:16, :] = sums[1]
+        for k in range(2):
+            red_x[t, 0, k : k + 1, :] = jnp.sum(sums[k], axis=0, keepdims=True)
         reduce_start(*over_x(t))
 
     def relay(t):
@@ -366,7 +366,7 @@
 
     def take_sums(t):
         both = reduce_end(*over_y(t))
-        return total(both[0:8]), total(both[8:16])
+        return total(both[0:1]), total(both[1:2])
 
     send_y(1, ys.at[0], lambda p: right_ref[p], side_s[4], side_n[4])
     scatter(diag, 0, ds_, dn_)
@@ -493,7 +493,7 @@
                 pltpu.VMEM((2, ny, nz), f32), pltpu.VMEM((2, nx, nz), f32),
                 pltpu.VMEM((2, ny, nz), f32), pltpu.VMEM((2, nx, nz), f32),
                 pltpu.VMEM((EXCHANGES, 2, ny, nz), f32), pltpu.VMEM((EXCHANGES, 2, nx, nz), f32),
-                pltpu.VMEM((2, ngx, 16, 128), f32), pltpu.VMEM((2, ngy, 16, 128), f32),
+                pltpu.VMEM((2, ngx, 2, 128), f32), pltpu.VMEM((2, ngy, 2, 128), f32),
                 pltpu.SemaphoreType.DMA((EXCHANGES, 6)), pltpu.SemaphoreType.DMA((EXCHANGES, 6)),
                 pltpu.SemaphoreType.DMA((2, ngx)), pltpu.SemaphoreType.DMA((2, ngx)),
                 pltpu.SemaphoreType.DMA((2, ngy)), pltpu.SemaphoreType.DMA((2, ngy)),

time: 44.2 us -> 43.9 us (level)
  no operation moved by 1% of the time
where the time goes in v6:
time: 43.9 us; the launch traced here: 43.7 us
  Pallas kernels  43.1 us (98%)
  between operations  0.64 us (1%)
    pallas_call x1, Pallas kernels, local(): pl.pallas_call(functools.partial(kernel, ngx, ngy), out_shape=[block] * 4...  41 us
    pallas_call x1, Pallas kernels, local(): pl.pallas_call(functools.partial(deliver, parts), out_shape=[jax.ShapeDty...  2.07 us

profile of v6, /device:TPU:0, one launch (start us, length us, event | category | flops | bytes accessed | tf_op | source)
XLA Modules:
  0.0 43.7 jit_solution(5277214335192704322)
XLA Ops:
  0.6 41.0 %shard_map.66 = (f32[32,32,256]{2,1,0:T(8,128)S(1)}, f32[32,32,256]{2,1,0:T(8,128)S(1)}, f32[32,32,256]{2,1,0:T(8,128)S(1)}, f32[32,32,256]{2,1,0:T(8,128)S(1)}) custom-call(f32[32,32,256]{2,1,0:T(8,128)} %right_in.1, s32[32,32,256]{2,1,0:T(8,128)} %phase_in.1, f32[4]{0:T(128)} %table_in.1), custom_call_target="tpu_custom_call" | custom-call | tf_op jit(solution)/shard_map/pallas_call | solution.py:482
  41.6 2.1 %shard_map.67 = (f32[32,32,256]{2,1,0:T(8,128)}, f32[32,32,256]{2,1,0:T(8,128)}, f32[32,32,256]{2,1,0:T(8,128)}, f32[32,32,256]{2,1,0:T(8,128)}) custom-call(f32[32,32,256]{2,1,0:T(8,128)S(1)} %get-tuple-element.8.refs_0_, f32[32,32,256]{2,1,0:T(8,128)S(1)} %get-tuple-element.9.refs_1_, f32[32,32,256]{2,1,0:T(8,128)S(1)} %get-tuple-element.10.refs_2_, ...), custom_call_target="tpu_custom_call" | custom-call | tf_op jit(solution)/shard_map/pallas_call | solution.py:507

commit v7 on v6

--- a/solution.py
+++ b/solution.py
@@ -31,7 +31,7 @@
 
 def loop(low, high, body, carry=None):
     count = high - low
-    unroll = next(u for u in (4, 5, 3, 2, 1) if count % u == 0)
+    unroll = next(u for u in (8, 6, 5, 4, 3, 2, 1) if count % u == 0)
 
     def step(k, value):
         for j in range(unroll):

time: 43.9 us -> 43.6 us (level)
  no operation moved by 1% of the time
where the time goes in v7:
time: 43.6 us; the launch traced here: 43.4 us
  Pallas kernels  42.8 us (98%)
  between operations  0.64 us (1%)
    pallas_call x1, Pallas kernels, local(): pl.pallas_call(functools.partial(kernel, ngx, ngy), out_shape=[block] * 4...  40.7 us
    pallas_call x1, Pallas kernels, local(): pl.pallas_call(functools.partial(deliver, parts), out_shape=[jax.ShapeDty...  2.07 us

profile of v7, /device:TPU:0, one launch (start us, length us, event | category | flops | bytes accessed | tf_op | source)
XLA Modules:
  0.0 43.4 jit_solution(11416877813616563016)
XLA Ops:
  0.6 40.7 %shard_map.66 = (f32[32,32,256]{2,1,0:T(8,128)S(1)}, f32[32,32,256]{2,1,0:T(8,128)S(1)}, f32[32,32,256]{2,1,0:T(8,128)S(1)}, f32[32,32,256]{2,1,0:T(8,128)S(1)}) custom-call(f32[32,32,256]{2,1,0:T(8,128)} %right_in.1, s32[32,32,256]{2,1,0:T(8,128)} %phase_in.1, f32[4]{0:T(128)} %table_in.1), custom_call_target="tpu_custom_call" | custom-call | tf_op jit(solution)/shard_map/pallas_call | solution.py:482
  41.4 2.1 %shard_map.67 = (f32[32,32,256]{2,1,0:T(8,128)}, f32[32,32,256]{2,1,0:T(8,128)}, f32[32,32,256]{2,1,0:T(8,128)}, f32[32,32,256]{2,1,0:T(8,128)}) custom-call(f32[32,32,256]{2,1,0:T(8,128)S(1)} %get-tuple-element.8.refs_0_, f32[32,32,256]{2,1,0:T(8,128)S(1)} %get-tuple-element.9.refs_1_, f32[32,32,256]{2,1,0:T(8,128)S(1)} %get-tuple-element.10.refs_2_, ...), custom_call_target="tpu_custom_call" | custom-call | tf_op jit(solution)/shard_map/pallas_call | solution.py:507
